TPU v7x, 128 devices: a whole 4x4x4 slice. The times are simulated.
128 devices in a mesh: tx: 8 (over y, core), ty: 16 (over z, x).
Axes of the slice: x: 4, y: 4, z: 4, core: 2. Of those that a mesh axis runs over, the one named last changes fastest.
Arguments:
- right_side: float32 [16, 256, 2048], P(None, 'tx', 'ty'), may hold values from -4 to 4
- screening: float32 [16, 256, 2048], P(None, 'tx', 'ty'), may hold values from 0.001 to 0.3
- owners: int32 [8, 16], P('tx'), may hold values from 0 to 15, as said below
Outputs:
- solution_field: float32 [16, 256, 2048], P(None, 'tx', 'ty')
- residual: float32 [16, 256, 2048], P(None, 'tx', 'ty')
Inputs may be any that keep to these rules, and one draw needn't show every extreme that they name: In each tile row the tile columns fall into runs of consecutive columns, each of 1 to 4 columns, the first run of every row holding exactly 4. All tiles of a run have the same entry of owners, and different runs of one row have different entries.
All inputs are finite; a program needn't handle non-finite values.
Results may differ from a plain program's by a relative error of at most 0.0003.
Values sent between devices are 32-bit elements; how exact they have to be, the bound alone decides.
A program may use at most 128 MiB of HBM per device.

v0:
```python
import jax
import jax.numpy as jnp
from jax import lax
from jax.sharding import PartitionSpec as P

ITERS = 2
LEVELS = 4
NU = 3
CS = 8
MOST = 4


OMEGA = 0.8


def extended_2(cells, sides, width):
    for axis, dim in sides:
        count = lax.axis_size(axis)
        ends = count - 1
        head = lax.slice_in_dim(cells, 0, width, axis=dim)
        tail = lax.slice_in_dim(cells, cells.shape[dim] - width, cells.shape[dim], axis=dim)
        cells = jnp.concatenate(
            [
                lax.ppermute(tail, axis, [(i, (i + 1) % count) for i in range(ends)]),
                cells,
                lax.ppermute(head, axis, [((i + 1) % count, i) for i in range(ends)]),
            ],
            axis=dim,
        )
    return cells


def restrict(values):
    depth, row_count, columns = values.shape
    blocks = values.reshape(depth // 2, 2, row_count // 2, 2, columns // 2, 2)
    return jnp.sum(blocks, axis=(1, 3, 5)) * 0.125


def prolong(values):
    return jnp.repeat(jnp.repeat(jnp.repeat(values, 2, axis=0), 2, axis=1), 2, axis=2)


def stencil_sum(extended, values):
    depth_padded = jnp.pad(values, ((1, 1), (0, 0), (0, 0)))
    summed = depth_padded[2:] + depth_padded[:-2]
    summed = summed + extended[:, 2:, 1:-1] + extended[:, :-2, 1:-1]
    return summed + extended[:, 1:-1, 2:] + extended[:, 1:-1, :-2]


def fine_stencil(values):
    extended = extended_2(values, (("tx", 1), ("ty", 2)), 1)
    return stencil_sum(extended, values)


def coarse_stencil(values):
    extended = extended_2(values, (("tx", 1), ("ty", 2)), 1)
    return stencil_sum(extended, values)


def strip_neighbours(values, column_links):
    depth_padded = jnp.pad(values, ((1, 1), (0, 0), (0, 0)))
    summed = depth_padded[2:] + depth_padded[:-2]
    row_padded = jnp.pad(values, ((0, 0), (1, 1), (0, 0)))
    summed = summed + row_padded[:, 2:, :] + row_padded[:, :-2, :]
    forward = values[:, :, 1:] * column_links
    backward = values[:, :, :-1] * column_links
    return (
        summed
        + jnp.pad(forward, ((0, 0), (0, 0), (0, 1)))
        + jnp.pad(backward, ((0, 0), (0, 0), (1, 0)))
    )


def strip_solve(source_row, screen_row, owner_row, run_start, coarse_cols, coupling):
    padding = ((0, 0), (0, 0), (0, MOST * coarse_cols))
    offset = run_start * coarse_cols
    source = lax.dynamic_slice_in_dim(jnp.pad(source_row, padding), offset, MOST * coarse_cols, 2)
    screen = lax.dynamic_slice_in_dim(jnp.pad(screen_row, padding), offset, MOST * coarse_cols, 2)
    padded_owners = jnp.concatenate([owner_row, jnp.full((MOST,), -1, jnp.int32)])
    block_owner = lax.dynamic_slice_in_dim(padded_owners, run_start, MOST)
    columns = jnp.repeat(block_owner, coarse_cols)
    column_links = (columns[1:] == columns[:-1]).astype(jnp.float32)
    diagonal = screen + 6.0 * coupling
    values = jnp.zeros_like(source)
    for counter in range(CS):
        nearby = strip_neighbours(values, column_links)
        values = values + OMEGA * (source - (diagonal * values - coupling * nearby)) / diagonal
    return values


def vcycle(source, screens, depth_level, coupling, coarse_solve):
    if depth_level == len(screens) - 1:
        return coarse_solve(source)
    screen = screens[depth_level]
    diagonal = screen + 6.0 * coupling
    stencil = fine_stencil if depth_level == 0 else coarse_stencil
    values = OMEGA * source / diagonal
    for counter in range(NU - 1):
        values = (
            values + OMEGA * (source - (diagonal * values - coupling * stencil(values))) / diagonal
        )
    defect = source - (diagonal * values - coupling * stencil(values))
    values = values + prolong(
        vcycle(restrict(defect), screens, depth_level + 1, 0.5 * coupling, coarse_solve)
    )
    for counter in range(NU):
        values = (
            values + OMEGA * (source - (diagonal * values - coupling * stencil(values))) / diagonal
        )
    return values


def inner_norm(first_vec, second_vec):
    return lax.psum(jnp.sum(first_vec * second_vec), ("tx", "ty"))


def on_device(right_side, screening, owners):
    screens = [screening]
    for counter in range(LEVELS - 1):
        screens.append(restrict(screens[-1]))
    column_index = lax.axis_index("ty")
    devices_ty = lax.axis_size("ty")
    owner_row = owners[0]
    leader = lax.dynamic_slice_in_dim(owner_row, column_index, 1)[0]
    places = jnp.arange(devices_ty, dtype=jnp.int32)
    owned_start = jnp.min(jnp.where(owner_row == column_index, places, devices_ty))
    coarse_cols = screens[-1].shape[2]
    coupling_last = 0.5 ** (LEVELS - 1)

    def coarse_solve(source):
        screen = screens[-1]
        chosen = (jnp.arange(devices_ty) == leader).astype(jnp.float32)
        spread = jnp.repeat(chosen, coarse_cols)
        outgoing_source = jnp.tile(source, (1, 1, devices_ty)) * spread
        outgoing_screen = jnp.tile(screen, (1, 1, devices_ty)) * spread
        gathered_source, gathered_screen = (
            lax.all_to_all(outgoing_source, "ty", split_axis=2, concat_axis=2, tiled=True),
            lax.all_to_all(outgoing_screen, "ty", split_axis=2, concat_axis=2, tiled=True),
        )
        solved = strip_solve(
            gathered_source, gathered_screen, owner_row, owned_start, coarse_cols, coupling_last
        )
        empty_row = jnp.zeros(solved.shape[:2] + ((devices_ty + MOST) * coarse_cols,), jnp.float32)
        placed = lax.dynamic_update_slice_in_dim(empty_row, solved, owned_start * coarse_cols, 2)[
            :, :, : devices_ty * coarse_cols
        ]
        owned_mask = jnp.repeat((owner_row == column_index).astype(jnp.float32), coarse_cols)
        returned = lax.all_to_all(
            placed * owned_mask, "ty", split_axis=2, concat_axis=2, tiled=True
        )
        return lax.dynamic_slice_in_dim(returned, leader * coarse_cols, coarse_cols, 2)

    solution_field = jnp.zeros_like(right_side)
    residual = right_side
    precond = vcycle(residual, screens, 0, 1.0, coarse_solve)
    direction = precond
    inner_now = inner_norm(residual, precond)
    for counter in range(ITERS):
        applied = (screening + 6.0) * direction - fine_stencil(direction)
        step_size = inner_now / lax.psum(jnp.sum(direction * applied), ("tx", "ty"))
        solution_field = solution_field + step_size * direction
        residual = residual - step_size * applied
        if counter + 1 < ITERS:
            precond = vcycle(residual, screens, 0, 1.0, coarse_solve)
            inner_next = inner_norm(residual, precond)
            direction = precond + inner_next / inner_now * direction
            inner_now = inner_next
    return (solution_field, residual)


def solution(mesh):
    in_specs = (P(None, "tx", "ty"), P(None, "tx", "ty"), P("tx", None))
    out_specs = (P(None, "tx", "ty"), P(None, "tx", "ty"))
    return jax.shard_map(
        on_device, mesh=mesh, in_specs=in_specs, out_specs=out_specs, check_vma=False
    )
```

profile of v0, /device:TPU:0, one launch (start us, length us, event | category | flops | bytes accessed | tf_op | source)
XLA Modules:
  0.0 1194.3 jit_solution(11418630638117046138)
XLA Ops:
  18.0 4.5 collective-permute-start.3
  39.1 4.9 collective-permute-start.7
  53.5 4.0 collective-permute-start.9
  62.6 4.8 collective-permute-start.11
  67.3 18.1 %reshape.115 = f32[8,2,16,2,64,2]{5,4,3,2,1,0:T(8,128)} reshape(f32[16,32,128]{2,1,0:T(8,128)S(1)} %copy-done.50) | data formatting | bytes 524288 | tf_op jit(solution)/shard_map/reshape | solution.py:35
  85.4 7.0 reduce_sum.118
  92.4 5.9 fusion.26
  99.9 18.1 %reshape.114 = f32[8,2,16,2,64,2]{5,4,3,2,1,0:T(8,128)} reshape(f32[16,32,128]{2,1,0:T(8,128)S(1)} %copy.1216) | data formatting | bytes 524288 | tf_op jit(solution)/shard_map/reshape | solution.py:35
  118.0 7.0 reduce_sum.117
  125.0 4.4 collective-permute-start.13
  135.3 4.6 collective-permute-start.15
  150.4 6.6 collective-permute-start.19
  168.1 7.6 collective-permute-start.23
  196.2 6.4 collective-permute-start.27
  212.4 7.2 collective-permute-start.31
  231.5 7.1 collective-permute-start.35
  245.3 16.8 %all-to-all-start = ((f32[16,1,128]{2,1,0:T(1,128)}), f32[16,1,128]{2,1,0:T(1,128)S(1)}, u32[]{:S(2)}, u32[]{:S(2)}) async-start(f32[16,1,128]{2,1,0:T(1,128)} %reshape.140), calls=%async_computation | async-start | bytes 16384 | tf_op jit(solution)/shard_map/all_to_all | solution.py:137
  264.2 5.4 all-to-all-done
  287.9 4.1 all-to-all-start.2
  292.7 6.8 all-to-all-done.2
  304.9 5.4 collective-permute-done.36
  311.7 4.5 collective-permute-start.39
  326.1 4.8 collective-permute-start.43
  340.8 4.8 collective-permute-start.47
  358.9 4.8 collective-permute-start.51
  374.2 4.9 collective-permute-start.55
  389.6 6.8 collective-permute-start.59
  407.3 4.0 collective-permute-start.61
  416.5 7.1 collective-permute-start.63
  440.2 7.0 collective-permute-start.67
  455.4 4.1 collective-permute-start.69
  464.8 7.0 collective-permute-start.71
  481.4 4.1 collective-permute-start.73
  490.7 6.9 collective-permute-start.75
  502.3 77.6 %all-reduce.102 = (f32[]{:T(128)}, f32[]{:T(128)}) all-reduce(f32[]{:T(128)} %get-tuple-element.15, f32[]{:T(128)} %get-tuple-element.14), channel_id=1, replica_groups=mesh['tx'=8,'ty'=16] {'tx','ty'}, use_global_device_ids=true, to_apply=%region_8.9 | all-reduce | flops 2 | bytes 16 | tf_op jit(solution)/shard_map/psum | solution.py:114
  595.9 4.5 collective-permute-start.79
  618.2 5.2 collective-permute-start.83
  624.4 5.9 fusion.82
  645.5 4.5 collective-permute-start.87
  656.8 18.8 %reshape.128 = f32[8,2,16,2,64,2]{5,4,3,2,1,0:T(8,128)} reshape(f32[16,32,128]{2,1,0:T(8,128)} %copy.1337) | data formatting | bytes 524288 | tf_op jit(solution)/shard_map/reshape | solution.py:35
  675.6 7.0 reduce_sum.125
  692.9 4.8 collective-permute-start.91
  708.7 5.2 collective-permute-start.95
  725.0 6.5 collective-permute-start.99
  747.7 7.1 collective-permute-start.103
  764.7 7.2 collective-permute-start.107
  781.8 7.1 collective-permute-start.111
  794.9 22.9 %all_to_all.26 = f32[16,1,128]{2,1,0:T(1,128)S(1)} all-to-all(f32[16,1,128]{2,1,0:T(1,128)S(1)} %reshape.146), channel_id=1, replica_groups=mesh['tx'=8,'ty'=16] {'ty'}, dimensions={0} | all-to-all | bytes 16384 | tf_op jit(solution)/shard_map/all_to_all | solution.py:137
  824.5 10.5 all_to_all.27
  840.5 4.2 collective-permute-done.112
  846.1 4.5 collective-permute-start.115
  860.5 4.8 collective-permute-start.119
  875.2 4.8 collective-permute-start.123
  893.3 4.8 collective-permute-start.127
  908.6 4.9 collective-permute-start.131
  924.0 6.8 collective-permute-start.135
  949.3 6.9 collective-permute-start.139
  973.4 7.0 collective-permute-start.143
  990.0 4.1 collective-permute-start.145
  999.3 7.1 collective-permute-start.147
  1007.8 7.8 multiply_reduce_fusion.1
  1015.6 76.6 %psum.30 = f32[]{:T(128)} all-reduce(f32[]{:T(128)} %get-tuple-element.20), channel_id=1, replica_groups=mesh['tx'=8,'ty'=16] {'tx','ty'}, use_global_device_ids=true, to_apply=%region_15.16 | all-reduce | flops 1 | bytes 8 | tf_op jit(solution)/shard_map/psum | solution.py:114
  1109.4 4.5 collective-permute-start.151
  1118.9 67.4 %psum.31 = f32[]{:T(128)} all-reduce(f32[]{:T(128)} %get-tuple-element.18), channel_id=1, replica_groups=mesh['tx'=8,'ty'=16] {'tx','ty'}, use_global_device_ids=true, to_apply=%region_17.18 | all-reduce | flops 1 | bytes 8 | tf_op jit(solution)/shard_map/psum | solution.py:160
  (748 shorter events, 543.2 us)
Async XLA Ops:
  50.6 7.0 collective-permute-start.8
  61.3 31.2 %collective-permute-start.10 = (f32[16,34,1]{1,0,2:T(8,128)S(1)}, f32[16,34,1]{1,0,2:T(8,128)S(1)}, u32[]{:S(2)}, u32[]{:S(2)}) collective-permute-start(f32[16,34,1]{1,0,2:T(8,128)S(1)} %get-tuple-element.47), channel_id=1, source_target_pairs={{1,0},{2,1},{3,2},{4,3},{5,4},{6,5},{7,6},{8,7},{9,8},{10,9},{11,1... | collective-permute-start | bytes 6536 | tf_op jit(solution)/shard_map/ppermute | solution.py:26
  62.6 29.9 %collective-permute-start.11 = (f32[16,34,1]{1,0,2:T(8,128)S(1)}, f32[16,34,1]{1,0,2:T(8,128)S(1)}, u32[]{:S(2)}, u32[]{:S(2)}) collective-permute-start(f32[16,34,1]{1,0,2:T(8,128)S(1)} %get-tuple-element.48), channel_id=1, source_target_pairs={{0,1},{1,2},{2,3},{3,4},{4,5},{5,6},{6,7},{7,8},{8,9},{9,10},{10,1... | collective-permute-start | bytes 6536 | tf_op jit(solution)/shard_map/ppermute | solution.py:24
  135.3 6.5 collective-permute-start.15
  149.1 8.3 collective-permute-start.18
  150.4 8.6 collective-permute-start.19
  166.8 14.2 %collective-permute-start.22 = (f32[8,18,1]{2,0,1:T(8,128)}, f32[8,18,1]{2,0,1:T(8,128)}, u32[]{:S(2)}, u32[]{:S(2)}) collective-permute-start(f32[8,18,1]{2,0,1:T(8,128)} %get-tuple-element.119), channel_id=1, source_target_pairs={{1,0},{2,1},{3,2},{4,3},{5,4},{6,5},{7,6},{8,7},{9,8},{10,9},{11,1... | collective-permute-start | bytes 1736 | tf_op jit(solution)/shard_map/ppermute | solution.py:26
  168.1 12.9 %collective-permute-start.23 = (f32[8,18,1]{2,0,1:T(8,128)}, f32[8,18,1]{2,0,1:T(8,128)}, u32[]{:S(2)}, u32[]{:S(2)}) collective-permute-start(f32[8,18,1]{2,0,1:T(8,128)} %get-tuple-element.120), channel_id=1, source_target_pairs={{0,1},{1,2},{2,3},{3,4},{4,5},{5,6},{6,7},{7,8},{8,9},{9,10},{10,1... | collective-permute-start | bytes 1736 | tf_op jit(solution)/shard_map/ppermute | solution.py:24
  194.5 8.7 collective-permute-start.26
  196.2 7.8 collective-permute-start.27
  211.1 8.5 collective-permute-start.30
  212.4 8.7 collective-permute-start.31
  221.3 8.8 collective-permute-start.33
  230.3 8.5 collective-permute-start.34
  231.5 8.6 collective-permute-start.35
  245.3 24.4 %all-to-all-start = ((f32[16,1,128]{2,1,0:T(1,128)}), f32[16,1,128]{2,1,0:T(1,128)S(1)}, u32[]{:S(2)}, u32[]{:S(2)}) async-start(f32[16,1,128]{2,1,0:T(1,128)} %reshape.140), calls=%async_computation | async-start | bytes 16384 | tf_op jit(solution)/shard_map/all_to_all | solution.py:137
  269.7 10.9 all-to-all-start.1
  287.9 11.5 all-to-all-start.2
  303.6 6.7 collective-permute-start.36
  357.6 6.5 collective-permute-start.50
  358.9 6.8 collective-permute-start.51
  372.9 6.6 collective-permute-start.54
  374.2 6.9 collective-permute-start.55
  388.3 8.5 collective-permute-start.58
  389.6 8.8 collective-permute-start.59
  404.3 7.1 collective-permute-start.60
  415.2 8.4 collective-permute-start.62
  416.5 8.3 collective-permute-start.63
  438.9 8.3 collective-permute-start.66
  440.2 8.4 collective-permute-start.67
  452.4 7.2 collective-permute-start.68
  463.4 8.4 collective-permute-start.70
  464.8 8.4 collective-permute-start.71
  478.5 7.1 collective-permute-start.72
  489.4 8.2 collective-permute-start.74
  490.7 8.1 collective-permute-start.75
  616.9 6.5 collective-permute-start.82
  633.6 6.8 collective-permute-start.84
  692.9 6.8 collective-permute-start.91
  707.4 6.9 collective-permute-start.94
  708.7 7.2 collective-permute-start.95
  723.7 8.2 collective-permute-start.98
  725.0 8.5 collective-permute-start.99
  746.4 8.4 collective-permute-start.102
  747.7 8.6 collective-permute-start.103
  763.4 8.5 collective-permute-start.106
  764.7 8.7 collective-permute-start.107
  780.5 8.4 collective-permute-start.110
  781.8 8.6 collective-permute-start.111
  892.1 6.5 collective-permute-start.126
  893.3 6.8 collective-permute-start.127
  907.3 6.6 collective-permute-start.130
  908.6 6.9 collective-permute-start.131
  922.7 8.5 collective-permute-start.134
  924.0 8.8 collective-permute-start.135
  937.1 7.1 collective-permute-start.136
  948.0 8.2 collective-permute-start.138
  949.3 8.3 collective-permute-start.139
  961.4 6.6 collective-permute-start.140
  971.9 8.4 collective-permute-start.142
  973.4 8.4 collective-permute-start.143
  987.1 7.1 collective-permute-start.144
  998.0 8.5 collective-permute-start.146
  999.3 8.5 collective-permute-start.147
  (143 other events, 1011.1 us)
where the time goes:
time: 1210 us; the launch traced here: 1190 us
  starting transfers between devices  474 us (39%)
  blocking collectives  255 us (21%)
  local copies, waits for them, and re-layouts  213 us (18%)
  waiting for transfers between devices  128 us (11%)
  other arithmetic  113 us (9%)
    ppermute x76, starting transfers between devices, extended_2(): lax.ppermute(tail, axis, [(i, (i + 1) % count) for i in range(ends)])  350 us
    psum x2, blocking collectives, inner_norm(): return lax.psum(jnp.sum(first_vec * second_vec), ('tx', 'ty'))  154 us
    ppermute x76, starting transfers between devices, extended_2(): lax.ppermute(head, axis, [((i + 1) % count, i) for i in range(ends)])  99.1 us
    psum x1, blocking collectives, on_device(): step_size = inner_now / lax.psum(jnp.sum(direction * applied), ('tx', 'ty'))  67.4 us
    reshape x7, local copies, waits for them, and re-layouts, restrict(): blocks = values.reshape(depth // 2, 2, row_count // 2, 2, columns // 2, 2)  63.7 us
    ppermute x76, waiting for transfers between devices, extended_2(): lax.ppermute(head, axis, [((i + 1) % count, i) for i in range(ends)])  61.6 us
    ppermute x76, waiting for transfers between devices, extended_2(): lax.ppermute(tail, axis, [(i, (i + 1) % count) for i in range(ends)])  50.7 us
    slice x28, local copies, waits for them, and re-layouts, extended_2(): lax.slice_in_dim(cells, cells.shape[dim] - width, cells.shape[dim], axis=...  44.3 us
  transfers between devices with their start and end apart: 155, of which 73 were waited for; matrix products, arithmetic and copies ran while one was open for 7% of the time, Pallas kernels for 0%

commit v1 on v0

v1 whole, which is shorter than its diff:
```python
import functools

import jax
import jax.numpy as jnp
from jax import lax
from jax.experimental import pallas as pl
from jax.experimental.pallas import tpu as pltpu
from jax.sharding import PartitionSpec as P

MESH = pl.DeviceIdType.MESH
F32 = jnp.float32
BF16 = jnp.bfloat16

NTX, NTY = 8, 16
HALO = 11
ROWS = 56
TOP = 12
PLANE = ROWS * 16
PITCH = 24
R1 = 32
DIRS8 = [(a, b) for a in (-1, 0, 1) for b in (-1, 0, 1) if (a, b) != (0, 0)]
DIRS14 = [(a, b) for a in (-2, -1, 0, 1, 2) for b in (-1, 0, 1) if (a, b) != (0, 0)]


def iota(shape, axis):
    return lax.broadcasted_iota(jnp.int32, shape, axis)


def dot_split(x, table):
    high = x.astype(BF16)
    low = (x - high.astype(F32)).astype(BF16)
    return jnp.dot(high, table, preferred_element_type=F32) + jnp.dot(
        low, table, preferred_element_type=F32
    )


def kernel(
    rhs_ref, scr_ref, own_ref, sol_ref, res_ref,
    bs1, b2, gain, va, vb, vc, q1, pk1, pk2, rp1, rp2, ebuf, xbuf,
    l1s, l1g, l1b, l1x, l1v, l1w, l1e,
    m1ud, m1lr, m2ud, m2lr, rt1, rt2,
    l2b, l2s, l2g, l2v, l2w, l2e, l2x,
    t01, p10, t12, u2, t23, p32, p21,
    arbuf, arr1, arr2,
    s_r1, r_r1, s_r2, r_r2, s_ar, r_ar,
):
    tx = lax.axis_index("tx")
    ty = lax.axis_index("ty")
    zero = lax.div(tx, 64)
    barrier = pltpu.get_barrier_semaphore()

    def inside(dx, dy):
        a, b = tx + dx, ty + dy
        return (a >= 0) & (a < NTX) & (b >= 0) & (b < NTY)

    def at(dx, dy):
        return {"tx": tx + dx, "ty": ty + dy}

    def ring(dx, dy):
        return {"tx": lax.rem(tx + dx, NTX), "ty": lax.rem(ty + dy, NTY)}

    ring_dirs = [(k, 0) for k in range(1, NTX)] + [(0, k) for k in range(1, NTY)]
    extra = [d for d in DIRS14 if d[0] != 0 and d[1] != 0]
    expected = jnp.int32(len(ring_dirs))
    for d in ring_dirs:
        pl.semaphore_signal(barrier, inc=1, device_id=ring(*d), device_id_type=MESH)
    for d in extra:
        ok = inside(*d)
        expected = expected + ok.astype(jnp.int32)

        @pl.when(ok)
        def _():
            pl.semaphore_signal(barrier, inc=1, device_id=at(*d), device_id_type=MESH)

    lane16 = iota((16, 128), 1)
    lane8 = iota((8, 128), 1)
    sub8 = iota((8, 128), 0)
    grp16 = lane16 >> 4
    grp8 = lane8 >> 4
    first16, last16 = lane16 == 0, lane16 == 127
    edge16 = (lane16 < 16) | (lane16 >= 112)
    side8 = ((lane8 >= 16) & (lane8 < 32)) | ((lane8 >= 96) & (lane8 < 112))
    z16 = jnp.zeros((16, 128), F32)
    z8 = jnp.zeros((8, 128), F32)

    def vrow(t, r):
        return pl.multiple_of(8 + (t * ROWS + r) * PITCH, 8)

    def brow(t, r):
        return pl.multiple_of((t * ROWS + r) * 16, 16)

    for z in range(16):
        for k in range(4):
            start = (TOP + 8 * k) * 16 + z
            bs1[0, pl.ds(start, 8, stride=16), :] = rhs_ref[z, 8 * k : 8 * k + 8, :]
            bs1[1, pl.ds(start, 8, stride=16), :] = scr_ref[z, 8 * k : 8 * k + 8, :]

    def pack0(src, count, pk):
        def body(j, c):
            for a in range(count):
                left, right = z16, z16
                for g in range(8):
                    x = src[a, pl.ds(brow(0, TOP + j * 8 + g), 16), :]
                    x = pltpu.roll(x, (16 * (g + 1)) % 128, 1)
                    right = jnp.where(grp16 == g, x, right)
                    left = jnp.where(grp16 == (g + 1) % 8, x, left)
                dst = pl.ds(pl.multiple_of(j * 16, 16), 16)
                pk[0, a, dst, :] = left
                pk[1, a, dst, :] = right
            return c

        lax.fori_loop(0, 4, body, 0)

    def unpack0(dst, count, rp, mask):
        def rows(dxi, j, groups):
            for a in range(count):
                span = pl.ds(pl.multiple_of(j * 16, 16), 16)
                fl = rp[dxi, 0, a, span, :]
                fr = rp[dxi, 1, a, span, :]
                for g in groups:
                    x = jnp.where(grp16 == g, fl, fr)
                    x = pltpu.roll(x, (128 - 16 * (g + 1)) % 128, 1)
                    if mask:
                        x = jnp.where(edge16, x, 0.0)
                    r = TOP + (dxi - 1) * 32 + j * 8 + g
                    dst[a, pl.ds(brow(1, r), 16), :] = x

        def body(j, c):
            rows(1, j, range(8))
            return c

        lax.fori_loop(0, 4, body, 0)
        rows(0, 2, range(5, 8))
        rows(0, 3, range(8))
        rows(2, 0, range(8))
        rows(2, 1, range(3))

    def r1_copy(i, d, src, pk, rp, cyc):
        dx, dy = d
        if dy == 0:
            if dx == -1:
                a, b = TOP, TOP + 32
            else:
                a, b = TOP + 32 - HALO, TOP - HALO
            s = src.at[:, pl.ds(a * 16, HALO * 16)]
            t = src.at[:, pl.ds(b * 16, HALO * 16)]
        else:
            side = 0 if dy == -1 else 1
            if dx == 0:
                s, t = pk.at[side], rp.at[1, 1 - side]
            elif dx == -1:
                s, t = pk.at[side, :, pl.ds(0, 32)], rp.at[2, 1 - side, :, pl.ds(0, 32)]
            else:
                s, t = pk.at[side, :, pl.ds(32, 32)], rp.at[0, 1 - side, :, pl.ds(32, 32)]
        return pltpu.make_async_remote_copy(
            src_ref=s, dst_ref=t, send_sem=s_r1.at[cyc, i], recv_sem=r_r1.at[cyc, i],
            device_id=at(*d), device_id_type=MESH,
        )

    def start_r1(src, pk, rp, cyc):
        for i, d in enumerate(DIRS8):
            @pl.when(inside(*d))
            def _():
                r1_copy(i, d, src, pk, rp, cyc).start()

    def wait_r1(src, pk, rp, cyc):
        for i, d in enumerate(DIRS8):
            @pl.when(inside(-d[0], -d[1]))
            def _():
                r1_copy(i, d, src, pk, rp, cyc).wait_recv()

    def sent_r1(src, pk, rp, cyc):
        for i, d in enumerate(DIRS8):
            @pl.when(inside(*d))
            def _():
                r1_copy(i, d, src, pk, rp, cyc).wait_send()

    def clear_r1(src, count, rp):
        for a in range(count):
            for t in (0, 1):
                for r in (0, ROWS - 1):
                    src[a, pl.ds(brow(t, r), 16), :] = z16
        for dx, r in ((-1, TOP - HALO), (1, TOP + 32)):
            @pl.when(jnp.logical_not(inside(dx, 0)))
            def _():
                for a in range(count):
                    src[a, pl.ds(r * 16, HALO * 16), :] = jnp.zeros((HALO * 16, 128), F32)
        for dxi in range(3):
            for sidei, dy in ((0, -1), (1, 1)):
                @pl.when(jnp.logical_not(inside(dxi - 1, dy)))
                def _():
                    rp[dxi, sidei] = jnp.zeros((count, 64, 128), F32)

    def r2_copy(i, d, mud, mlr, rt, cyc):
        dx, dy = d
        ns = 2 - cyc
        if dy == 0:
            n = (6 + ns - cyc) if abs(dx) == 1 else ns
            s = mud.at[0 if dx < 0 else 1, pl.ds(0, n)]
        else:
            n = (2 + ns) if abs(dx) <= 1 else ns
            s = mlr.at[0 if dy < 0 else 1, pl.ds(0, n)]
        return pltpu.make_async_remote_copy(
            src_ref=s, dst_ref=rt.at[2 - dx, 1 - dy, pl.ds(0, n)],
            send_sem=s_r2.at[cyc, i], recv_sem=r_r2.at[cyc, i],
            device_id=at(*d), device_id_type=MESH,
        )

    def each_r2(op, mud, mlr, rt, cyc):
        for i, d in enumerate(DIRS14):
            @pl.when(inside(-d[0], -d[1]) if op == "wait_recv" else inside(*d))
            def _():
                getattr(r2_copy(i, d, mud, mlr, rt, cyc), op)()

    def clear_r2(rt):
        for dx, dy in DIRS14:
            @pl.when(jnp.logical_not(inside(dx, dy)))
            def _():
                rt[2 + dx, 1 + dy] = jnp.zeros((8, 8, 128), F32)

    def ar_copy(cyc, i):
        if i < 7:
            d, s, t = ring(i + 1, 0), arbuf.at[cyc, 0], arr1.at[cyc, i]
        else:
            d, s, t = ring(0, i - 6), arbuf.at[cyc, 1], arr2.at[cyc, i - 7]
        return pltpu.make_async_remote_copy(
            src_ref=s, dst_ref=t, send_sem=s_ar.at[cyc, i], recv_sem=r_ar.at[cyc, i],
            device_id=d, device_id_type=MESH,
        )

    def ar_begin(cyc, rows):
        out = z8
        for k, acc in enumerate(rows):
            out = jnp.where(sub8 == k, jnp.sum(acc, axis=0, keepdims=True), out)
        arbuf[cyc, 0] = out
        for i in range(7):
            ar_copy(cyc, i).start()

    def ar_middle(cyc):
        total = arbuf[cyc, 0]
        for i in range(7):
            ar_copy(cyc, i).wait_recv()
        for i in range(7):
            total = total + arr1[cyc, i]
        arbuf[cyc, 1] = total
        for i in range(7, 22):
            ar_copy(cyc, i).start()

    def ar_end(cyc, count):
        total = arbuf[cyc, 1]
        for i in range(7, 22):
            ar_copy(cyc, i).wait_recv()
        for i in range(15):
            total = total + arr2[cyc, i]
        sums = jnp.broadcast_to(jnp.sum(total, axis=1, keepdims=True), (8, 128))
        return [jnp.broadcast_to(sums[k : k + 1], (8, 128)) for k in range(count)]

    def stencil0(src, r, count, tiles, with_centre):
        rows = [
            [src[pl.ds(vrow(t, r + k - 1), 16), :] for k in range(count + 2)] for t in (0, 1)
        ]
        for k in range(count):
            c = [rows[0][k + 1], rows[1][k + 1]]
            left = [pltpu.roll(x, 1, 1) for x in c]
            right = [pltpu.roll(x, 127, 1) for x in c]
            for t in tiles:
                at_row = vrow(t, r + k)
                n = rows[t][k] + rows[t][k + 2]
                n = n + (src[pl.ds(at_row - 1, 16), :] + src[pl.ds(at_row + 1, 16), :])
                n = n + jnp.where(first16, left[1 - t], left[t])
                n = n + jnp.where(last16, right[1 - t], right[t])
                with_centre(k, t, c[t], n)

    def sweep0(src, dst, bref, r0, steps):
        def body(i, carry):
            r = r0 + 4 * i

            def put(k, t, c, n):
                row = pl.ds(brow(t, r + k), 16)
                dst[pl.ds(vrow(t, r + k), 16), :] = 0.2 * c + gain[row, :] * (bref[0, row, :] + n)

            stencil0(src, r, 4, (0, 1), put)
            return carry

        lax.fori_loop(0, steps, body, 0)

    def restrict0(out):
        for i in range(3):
            parts = []
            for t in (0, 1):
                parts.append(
                    ebuf[t, pl.ds(i * 128, 64, stride=2), :]
                    + ebuf[t, pl.ds(i * 128 + 1, 64, stride=2), :]
                )
            x = jnp.concatenate(parts, axis=1)
            out[pl.ds(32 + i * 64, 64), :] = dot_split(x, t01[...])

    def wrow(r):
        return pl.multiple_of(8 + r * 16, 8)

    def stencil1(src, r, count, put):
        rows = [src[pl.ds(wrow(r + k - 1), 8), :] for k in range(count + 2)]
        for k in range(count):
            c = rows[k + 1]
            n = rows[k] + rows[k + 2]
            n = n + (src[pl.ds(wrow(r + k) - 1, 8), :] + src[pl.ds(wrow(r + k) + 1, 8), :])
            n = n + (pltpu.roll(c, 1, 1) + pltpu.roll(c, 127, 1))
            put(k, c, n)

    def sweep1(src, dst):
        def body(i, carry):
            r = 4 + 8 * i

            def put(k, c, n):
                row = pl.ds(pl.multiple_of((r + k) * 8, 8), 8)
                dst[pl.ds(wrow(r + k), 8), :] = 0.2 * c + l1g[row, :] * (l1b[row, :] + 0.5 * n)

            stencil1(src, r, 8, put)
            return carry

        lax.fori_loop(0, 3, body, 0)

    def restrict1():
        parts = []
        for z in range(4):
            x = l1e[pl.ds(2 * z, 8, stride=16), :] + l1e[pl.ds(2 * z + 1, 8, stride=16), :]
            x = x + l1e[pl.ds(2 * z + 8, 8, stride=16), :] + l1e[pl.ds(2 * z + 9, 8, stride=16), :]
            parts.append(x)
        return dot_split(jnp.concatenate(parts, axis=1), t12[...])

    def base2(z, k):
        return z * 56 + 8 + 8 * k + zero

    def stencil2(src, z, k):
        c = src[pl.ds(base2(z, k), 8), :]
        n = src[pl.ds(base2(z, k) - 1, 8), :] + src[pl.ds(base2(z, k) + 1, 8), :]
        if z > 0:
            n = n + src[pl.ds(base2(z - 1, k), 8), :]
        if z < 3:
            n = n + src[pl.ds(base2(z + 1, k), 8), :]
        return c, n + (pltpu.roll(c, 1, 1) + pltpu.roll(c, 127, 1))

    def sweep2(src, dst, tiles):
        for z in range(4):
            for k in tiles:
                c, n = stencil2(src, z, k)
                row = pl.ds(z * 40 + 8 * k, 8)
                dst[pl.ds(base2(z, k), 8), :] = 0.2 * c + l2g[row, :] * (l2b[row, :] + 0.25 * n)

    def table(ref, rows, cols, f):
        ref[...] = jnp.where(f(iota((rows, cols), 0), iota((rows, cols), 1)), ref_scale[0], 0.0).astype(BF16)

    ref_scale = [0.125]

    def col0(k):
        return jnp.where(k < 128, k, jnp.where(k < 192, k, k - 256))

    table(t01, 256, 128, lambda i, o: (col0(i) >> 1) == o - 32)
    table(t12, 512, 128, lambda i, o: (((i & 127) - 32) >> 1 == (o & 31)) & ((i >> 7) == (o >> 5)))
    table(t23, 128, 128, lambda i, o: ((i - 48) >> 1) == o - 56)
    ref_scale[0] = 1.0
    table(p10, 128, 256, lambda i, o: (col0(o) >> 1) == i - 32)
    table(u2, 384, 512, lambda i, o: (((i & 127) >> 5) == (o >> 7)) & ((o & 127) - 48 == ((i >> 7) - 1) * 32 + (i & 31)))
    table(p32, 128, 128, lambda i, o: ((o - 48) >> 1) == i - 56)
    table(p21, 128, 128, lambda i, o: ((o - 32) >> 1) == i - 48)

    def clear_pads(i, c):
        for ref in (va, vb, vc):
            ref[pl.ds(pl.multiple_of(i * PITCH, 8), 8), :] = z8
        return c

    lax.fori_loop(0, 2 * ROWS + 1, clear_pads, 0)
    for ref in (vb, vc):
        for t in (0, 1):
            for r in (0, 1, ROWS - 2, ROWS - 1):
                ref[pl.ds(vrow(t, r), 16), :] = z16
    for ref in (l1v, l1w):
        ref[...] = jnp.zeros(ref.shape, F32)
    for ref in (l1s, l1g, l1b):
        ref[...] = jnp.zeros(ref.shape, F32)
    for ref in (l2v, l2w):
        ref[...] = jnp.zeros(ref.shape, F32)
    clear_r1(bs1, 2, rp1)
    clear_r1(b2, 1, rp2)
    clear_r2(rt1)
    clear_r2(rt2)

    here = own_ref[0, ty]
    link_l = jnp.where(own_ref[0, jnp.maximum(ty - 1, 0)] == here, 1.0, 0.0)
    link_r = jnp.where(own_ref[0, jnp.minimum(ty + 1, NTY - 1)] == here, 1.0, 0.0)
    link = jnp.where(lane8 == 56, link_l, jnp.where(lane8 == 72, link_r, 1.0))

    pack0(bs1, 2, pk1)
    pl.semaphore_wait(barrier, expected)
    start_r1(bs1, pk1, rp1, 0)

    level3 = {}

    def vcycle(cyc, src, pk, rp, mud, mlr, rt, x, y):
        ns = 2 - cyc
        wait_r1(src, pk, rp, cyc)
        unpack0(src, ns, rp, cyc == 0)

        def start0(i, c):
            for k in range(4):
                for t in (0, 1):
                    row = pl.ds(brow(t, 4 * i + k), 16)
                    if cyc == 0:
                        s = bs1[1, row, :]
                        g = jnp.where(s > 0.0, 0.8 / (s + 6.0), 0.0)
                        gain[row, :] = g
                    else:
                        g = gain[row, :]
                    x[pl.ds(vrow(t, 4 * i + k), 16), :] = g * src[0, row, :]
            return c

        lax.fori_loop(0, ROWS // 4, start0, 0)
        if cyc == 0:
            def sum_rows(i, c):
                for t in (0, 1):
                    ebuf[t, pl.ds(pl.multiple_of(i * 16, 16), 16), :] = (
                        bs1[1, pl.ds(brow(t, 4 + 2 * i), 16), :]
                        + bs1[1, pl.ds(brow(t, 5 + 2 * i), 16), :]
                    )
                return c

            lax.fori_loop(0, 24, sum_rows, 0, unroll=4)
            restrict0(l1s)
            s = l1s[...]
            l1g[...] = jnp.where(s > 0.0, 0.8 / (s + 3.0), 0.0)
            l1e[...] = l1s[pl.ds(64, 128), :]
            s2_own = restrict1()

        sweep0(x, y, src, 2, 13)
        sweep0(y, x, src, 2, 13)

        def defect0(i, c):
            r = 4 + 4 * i
            held = {}

            def put(k, t, centre, n):
                row = pl.ds(brow(t, r + k), 16)
                held[k, t] = src[0, row, :] - (bs1[1, row, :] + 6.0) * centre + n
                if k % 2 == 1:
                    ebuf[t, pl.ds(pl.multiple_of((2 * i + k // 2) * 16, 16), 16), :] = (
                        held[k - 1, t] + held[k, t]
                    )

            stencil0(x, r, 4, (0, 1), put)
            return c

        lax.fori_loop(0, 12, defect0, 0)
        restrict0(l1b)

        for r in range(4, 28):
            row = pl.ds(r * 8, 8)
            l1v[pl.ds(wrow(r), 8), :] = l1g[row, :] * l1b[row, :]
        sweep1(l1v, l1w)
        sweep1(l1w, l1v)

        def defect1(i, c):
            r = 8 + 8 * i

            def put(k, centre, n):
                row = pl.ds(pl.multiple_of((r + k) * 8, 8), 8)
                l1e[pl.ds(pl.multiple_of((8 * i + k) * 8, 8), 8), :] = (
                    l1b[row, :] - (l1s[row, :] + 3.0) * centre + 0.5 * n
                )

            stencil1(l1v, r, 8, put)
            return c

        lax.fori_loop(0, 2, defect1, 0)
        b2_own = restrict1()

        for m in (0, 1):
            mud[m, 0] = b2_own
            mlr[m, 0] = b2_own
            if cyc == 0:
                mud[m, 1] = s2_own
                mlr[m, 1] = s2_own
                mud[m, 7] = link
            for k in range(5):
                mud[m, ns + k] = l1v[pl.ds(wrow(8 + k + 11 * m), 8), :]
        for j in (0, 1):
            left, right = z8, z8
            for g in range(8):
                v = pltpu.roll(l1v[pl.ds(wrow(8 + 8 * j + g), 8), :], (16 * g - 80) % 128, 1)
                right = jnp.where(grp8 == g, v, right)
                left = jnp.where(grp8 == (g + 5) % 8, v, left)
            mlr[0, ns + j] = left
            mlr[1, ns + j] = right
        each_r2("start", mud, mlr, rt, cyc)
        rt[2, 1, 0] = b2_own
        if cyc == 0:
            rt[2, 1, 1] = s2_own
        each_r2("wait_recv", mud, mlr, rt, cyc)

        blocks = []
        for a in range(ns):
            blocks.append(
                jnp.concatenate(
                    [
                        jnp.concatenate([rt[dxi, dyi, a] for dxi in range(5)], axis=0)
                        for dyi in range(3)
                    ],
                    axis=1,
                )
            )
        for a in range(ns):
            spread = dot_split(blocks[a], u2[...])
            for z in range(4):
                part = spread[:, 128 * z : 128 * z + 128]
                if a == 0:
                    l2b[pl.ds(z * 40, 40), :] = part
                else:
                    l2s[pl.ds(z * 40, 40), :] = part
        if cyc == 0:
            s = l2s[...]
            l2g[...] = jnp.where(s > 0.0, 0.8 / (s + 1.5), 0.0)
            for z in range(2):
                l2e[pl.ds(z * 40, 40), :] = (
                    l2s[pl.ds(2 * z * 40, 40), :] + l2s[pl.ds((2 * z + 1) * 40, 40), :]
                )
            level3["s"] = restrict2()
            s = level3["s"]
            level3["g"] = jnp.where(s > 0.0, 0.8 / (s + 0.75), 0.0)
            up, down = rt[1, 1, 7], rt[3, 1, 7]
            ml = [jnp.where(sub8 < 4, up, link), down]
            level3["ml"] = [0.125 * m for m in ml]
            level3["mr"] = [pltpu.roll(0.125 * m, 127, 1) for m in ml]
        for z in range(4):
            for k in range(5):
                row = pl.ds(z * 40 + 8 * k, 8)
                l2v[pl.ds(base2(z, k), 8), :] = l2g[row, :] * l2b[row, :]
        sweep2(l2v, l2w, range(5))
        sweep2(l2w, l2v, range(5))
        for k in range(5):
            d = []
            for z in range(4):
                c, n = stencil2(l2v, z, k)
                row = pl.ds(z * 40 + 8 * k, 8)
                d.append(l2b[row, :] - (l2s[row, :] + 1.5) * c + 0.25 * n)
            l2e[pl.ds(8 * k, 8), :] = d[0] + d[1]
            l2e[pl.ds(40 + 8 * k, 8), :] = d[2] + d[3]
        b3 = restrict2()
        solve3(b3)

        for z in range(4):
            for k in (1, 2, 3):
                row = pl.ds(base2(z, k), 8)
                l2v[row, :] = l2v[row, :] + l2x[pl.ds((z // 2) * 32 + 8 * (k - 1), 8), :]
        sweep2(l2v, l2w, (1, 2, 3))
        sweep2(l2w, l2v, (1, 2, 3))
        sweep2(l2v, l2w, (1, 2, 3))
        e2 = jnp.concatenate([l2w[pl.ds(z * 56 + 20 + zero, 16), :] for z in range(4)], axis=0)
        e2 = dot_split(e2, p21[...])
        for z in range(4):
            for a in (0, 8):
                for b in (0, 1):
                    l1x[pl.ds(a + 2 * z + b, 16, stride=16), :] = e2[16 * z : 16 * z + 16]

        for r in range(3, 29):
            tile, inner = (r - 8) // 16, (r - 8) % 16
            j, g = inner // 8, inner % 8
            v = jnp.where(grp8 == g, rt[2 + tile, 0, ns + j], rt[2 + tile, 2, ns + j])
            v = pltpu.roll(v, (16 - 16 * g) % 128, 1)
            if tile == 0:
                base = l1v[pl.ds(wrow(r), 8), :]
            elif tile < 0:
                base = rt[1, 1, ns + inner - 11]
            else:
                base = rt[3, 1, ns + inner]
            l1v[pl.ds(wrow(r), 8), :] = jnp.where(side8, v, base) + l1x[pl.ds(r * 8, 8), :]
        sweep1(l1v, l1w)
        sweep1(l1w, l1v)
        sweep1(l1v, l1w)
        for i in range(2):
            e1 = jnp.concatenate([l1w[pl.ds(wrow(6 + 10 * i + k), 8), :] for k in range(10)], axis=0)
            e1 = dot_split(e1, p10[...])
            for t in (0, 1):
                for b in (0, 1):
                    xbuf[t, pl.ds(160 * i + b, 80, stride=2), :] = e1[:, 128 * t : 128 * t + 128]

        def correct0(i, c):
            for t in (0, 1):
                e = xbuf[t, pl.ds(pl.multiple_of(i * 16, 16), 16), :]
                for k in (0, 1):
                    row = pl.ds(vrow(t, 8 + 2 * i + k), 16)
                    x[row, :] = x[row, :] + e
            return c

        lax.fori_loop(0, 20, correct0, 0, unroll=2)
        sweep0(x, y, src, 8, 10)
        sweep0(y, x, src, 10, 9)
        sweep0(x, y, src, 10, 9)

    def restrict2():
        parts = [
            l2e[pl.ds(z * 40 + 8, 16, stride=2), :] + l2e[pl.ds(z * 40 + 9, 16, stride=2), :]
            for z in range(2)
        ]
        return dot_split(jnp.concatenate(parts, axis=0), t23[...])

    def solve3(b3):
        up_ok = jnp.where((sub8 & 3) != 0, 0.125, 0.0)
        down_ok = jnp.where((sub8 & 3) != 3, 0.125, 0.0)
        g = [[level3["g"][16 * z + 8 * k : 16 * z + 8 * k + 8] for k in (0, 1)] for z in (0, 1)]
        b = [[b3[16 * z + 8 * k : 16 * z + 8 * k + 8] for k in (0, 1)] for z in (0, 1)]
        v = [[g[z][k] * b[z][k] for k in (0, 1)] for z in (0, 1)]
        for counter in range(7):
            new = [[None, None], [None, None]]
            for z in (0, 1):
                for k in (0, 1):
                    c = v[z][k]
                    n = 0.125 * v[1 - z][k]
                    n = n + pltpu.roll(c, 1, 0) * up_ok + pltpu.roll(c, 7, 0) * down_ok
                    n = n + pltpu.roll(c, 1, 1) * level3["ml"][k] + pltpu.roll(c, 127, 1) * level3["mr"][k]
                    new[z][k] = 0.2 * c + g[z][k] * (b[z][k] + n)
            v = new
        e3 = jnp.concatenate([v[0][0], v[0][1], v[1][0], v[1][1]], axis=0)
        e3 = dot_split(e3, p32[...])
        for z in (0, 1):
            for a in (0, 1):
                l2x[pl.ds(z * 32 + a, 16, stride=2), :] = e3[16 * z : 16 * z + 16]

    vcycle(0, bs1, pk1, rp1, m1ud, m1lr, rt1, va, vb)

    def halves(a):
        return a[0:8] + a[8:16]

    def apply_first(i, acc):
        r = TOP + 4 * i
        rz, zq = acc
        held = []

        def put(k, t, c, n):
            row = pl.ds(brow(0, r + k), 16)
            q = (bs1[1, row, :] + 6.0) * c - n
            b2[0, row, :] = q
            held.append((bs1[0, row, :] * c, c * q))

        stencil0(vb, r, 4, (0,), put)
        for a, b in held:
            rz = rz + halves(a)
            zq = zq + halves(b)
        return rz, zq

    sums = lax.fori_loop(0, 8, apply_first, (z8, z8))
    pack0(b2, 1, pk2)
    start_r1(b2, pk2, rp2, 1)
    ar_begin(0, sums)
    ar_middle(0)

    vcycle(1, b2, pk2, rp2, m2ud, m2lr, rt2, va, vc)
    rho0, curv0 = ar_end(0, 2)
    step0 = rho0 / curv0
    step0_16 = jnp.concatenate([step0, step0], axis=0)

    def next_z(i, c):
        for k in (0, 1):
            for t in (0, 1):
                row = pl.ds(vrow(t, TOP - 2 + 2 * i + k), 16)
                vc[row, :] = vb[row, :] - step0_16 * vc[row, :]
        return c

    lax.fori_loop(0, 18, next_z, 0, unroll=2)

    def apply_second(i, acc):
        r = TOP + 4 * i
        rz, zz, cross = acc
        held = []

        def put(k, t, c, n):
            row = pl.ds(brow(0, r + k), 16)
            q = (bs1[1, row, :] + 6.0) * c - n
            q1[row, :] = q
            q0 = b2[0, row, :]
            z0 = vb[pl.ds(vrow(0, r + k), 16), :]
            held.append(((bs1[0, row, :] - step0_16 * q0) * c, c * q, c * q0 + z0 * q))

        stencil0(vc, r, 4, (0,), put)
        for a, b, d in held:
            rz, zz, cross = rz + halves(a), zz + halves(b), cross + halves(d)
        return rz, zz, cross

    sums = lax.fori_loop(0, 8, apply_second, (z8, z8, z8))
    ar_begin(1, sums)
    ar_middle(1)
    rho1, zz, cross = ar_end(1, 3)
    beta = rho1 / rho0
    curv1 = zz + beta * (cross + beta * curv0)
    step1 = rho1 / curv1
    mixed = step0 + step1 * beta

    for z in range(16):
        for k in range(4):
            r = TOP + 8 * k
            z0 = vb[pl.ds(8 + r * PITCH + z, 8, stride=PITCH), :]
            z1 = vc[pl.ds(8 + r * PITCH + z, 8, stride=PITCH), :]
            q0 = b2[0, pl.ds(r * 16 + z, 8, stride=16), :]
            qn = q1[pl.ds(r * 16 + z, 8, stride=16), :]
            sol_ref[z, 8 * k : 8 * k + 8, :] = mixed * z0 + step1 * z1
            res_ref[z, 8 * k : 8 * k + 8, :] = rhs_ref[z, 8 * k : 8 * k + 8, :] - mixed * q0 - step1 * qn

    sent_r1(bs1, pk1, rp1, 0)
    sent_r1(b2, pk2, rp2, 1)
    each_r2("wait_send", m1ud, m1lr, rt1, 0)
    each_r2("wait_send", m2ud, m2lr, rt2, 1)
    for cyc in (0, 1):
        for i in range(22):
            ar_copy(cyc, i).wait_send()


def on_device(right_side, screening, owners):
    vm = lambda *s: pltpu.VMEM(s, F32)
    bm = lambda *s: pltpu.VMEM(s, BF16)
    padded = 8 + 2 * ROWS * PITCH + 8
    scratch = [
        vm(2, 2 * PLANE, 128), vm(1, 2 * PLANE, 128), vm(2 * PLANE, 128),
        vm(padded, 128), vm(padded, 128), vm(padded, 128), vm(PLANE, 128),
        vm(2, 2, 64, 128), vm(2, 1, 64, 128), vm(3, 2, 2, 64, 128), vm(3, 2, 1, 64, 128),
        vm(2, 24 * 16, 128), vm(2, 20 * 16, 128),
        vm(R1 * 8, 128), vm(R1 * 8, 128), vm(R1 * 8, 128), vm(R1 * 8, 128),
        vm(R1 * 16 + 16, 128), vm(R1 * 16 + 16, 128), vm(128, 128),
        vm(2, 8, 8, 128), vm(2, 4, 8, 128), vm(2, 8, 8, 128), vm(2, 4, 8, 128),
        vm(5, 3, 8, 8, 128), vm(5, 3, 8, 8, 128),
        vm(160, 128), vm(160, 128), vm(160, 128), vm(4 * 56, 128), vm(4 * 56, 128),
        vm(80, 128), vm(64, 128),
        bm(256, 128), bm(128, 256), bm(512, 128), bm(384, 512), bm(128, 128), bm(128, 128), bm(128, 128),
        vm(2, 2, 8, 128), vm(2, 7, 8, 128), vm(2, 15, 8, 128),
        pltpu.SemaphoreType.DMA((2, 8)), pltpu.SemaphoreType.DMA((2, 8)),
        pltpu.SemaphoreType.DMA((2, 14)), pltpu.SemaphoreType.DMA((2, 14)),
        pltpu.SemaphoreType.DMA((2, 22)), pltpu.SemaphoreType.DMA((2, 22)),
    ]
    block = jax.ShapeDtypeStruct(right_side.shape, F32)
    vmem = pl.BlockSpec(memory_space=pltpu.VMEM)
    return tuple(
        pl.pallas_call(
            kernel,
            out_shape=(block, block),
            in_specs=[vmem, vmem, pl.BlockSpec(memory_space=pltpu.SMEM)],
            out_specs=(vmem, vmem),
            scratch_shapes=scratch,
            compiler_params=pltpu.CompilerParams(
                collective_id=0, has_side_effects=True, vmem_limit_bytes=40 * 2**20
            ),
        )(right_side, screening, owners)
    )


def solution(mesh):
    spec = P(None, "tx", "ty")
    return jax.shard_map(
        on_device, mesh=mesh, in_specs=(spec, spec, P("tx", None)), out_specs=(spec, spec),
        check_vma=False,
    )
```

time: 1210 us -> 69.2 us (0.06); the launches traced: 1190 us -> 68.8 us
  starting transfers between devices: 474 us -> 0 us
  blocking collectives: 255 us -> 0 us
  local copies, waits for them, and re-layouts: 213 us -> 3.95 us
  waiting for transfers between devices: 128 us -> 0 us
  other arithmetic: 113 us -> 0 us
  Pallas kernels: 0 us -> 64.1 us
    ppermute x152 -> x0, starting transfers between devices: 449 us -> none  [the longest x76 350 us: extended_2(): lax.ppermute(tail, axis, [(i, (i + 1) % count) for i in range(ends)])]
    psum x3 -> x0, blocking collectives: 222 us -> none  [the longest x2 154 us: inner_norm(): return lax.psum(jnp.sum(first_vec * second_vec), ('tx', 'ty'))]
    ppermute x152 -> x0, waiting for transfers between devices: 112 us -> none  [the longest x76 61.6 us: extended_2(): lax.ppermute(head, axis, [((i + 1) % count, i) for i in range(ends)])]
    reshape x18 -> x0, local copies, waits for them, and re-layouts: 71.2 us -> none  [the longest x7 63.7 us: restrict(): blocks = values.reshape(depth // 2, 2, row_count // 2, 2, columns // 2, 2)]
    pallas_call x0 -> x1, Pallas kernels: none -> 64.1 us  [on_device(): pl.pallas_call(kernel, out_shape=(block, block), in_specs=[vmem, vmem, pl...]
    slice x90 -> x0, local copies, waits for them, and re-layouts: 61.5 us -> none  [the longest x28 44.3 us: extended_2(): lax.slice_in_dim(cells, cells.shape[dim] - width, cells.shape[dim], axis=...]
    reduce_sum x12 -> x0, other arithmetic: 44.5 us -> none  [the longest x9 29.6 us: restrict(): return jnp.sum(blocks, axis=(1, 3, 5)) * 0.125]
    ppermute x28 -> x0, local copies, waits for them, and re-layouts: 40 us -> none  [the longest x14 20.1 us: extended_2(): lax.ppermute(tail, axis, [(i, (i + 1) % count) for i in range(ends)])]
  transfers between devices with their start and end apart: 155 -> 0, of which waited for: 73 -> 0; matrix products, arithmetic and copies ran while one was open for 7% -> 0% of each run, Pallas kernels for 0% -> 0%
where the time goes in v1:
time: 69.2 us; the launch traced here: 68.8 us
  Pallas kernels  64.1 us (93%)
  local copies, waits for them, and re-layouts  3.95 us (6%)
    pallas_call x1, Pallas kernels, on_device(): pl.pallas_call(kernel, out_shape=(block, block), in_specs=[vmem, vmem, pl...  64.1 us
    unnamed x8, local copies, waits for them, and re-layouts  3.95 us

profile of v1, /device:TPU:0, one launch (start us, length us, event | category | flops | bytes accessed | tf_op | source)
XLA Modules:
  0.0 68.8 jit_solution(18238710749558588584)
XLA Ops:
  0.6 0.0 copy-start
  0.6 0.9 %copy-done = f32[16,32,128]{2,1,0:T(8,128)S(1)} copy-done((f32[16,32,128]{2,1,0:T(8,128)S(1)}, f32[16,32,128]{2,1,0:T(8,128)}, u32[]{:S(2)}) %copy-start) | copy-done | bytes 262168
  1.6 0.0 copy-start.1
  1.6 0.9 %copy-done.1 = f32[16,32,128]{2,1,0:T(8,128)S(1)} copy-done((f32[16,32,128]{2,1,0:T(8,128)S(1)}, f32[16,32,128]{2,1,0:T(8,128)}, u32[]{:S(2)}) %copy-start.1) | copy-done | bytes 262168
  2.5 0.0 copy-start.2
  2.5 0.7 copy-done.2
  3.2 64.1 %shard_map.50 = (f32[16,32,128]{2,1,0:T(8,128)S(1)}, f32[16,32,128]{2,1,0:T(8,128)S(1)}) custom-call(f32[16,32,128]{2,1,0:T(8,128)S(1)} %copy-done, f32[16,32,128]{2,1,0:T(8,128)S(1)} %copy-done.1, s32[1,16]{1,0:T(1,128)S(1)} %copy-done.2), custom_call_target="tpu_custom_call" | custom-call | tf_op jit(solution)/shard_map/pallas_call | solution.py:739
  67.3 0.7 %copy.7 = f32[16,32,128]{2,1,0:T(8,128)} copy(f32[16,32,128]{2,1,0:T(8,128)S(1)} %get-tuple-element.4) | data formatting | bytes 524288
  68.1 0.7 %copy.8 = f32[16,32,128]{2,1,0:T(8,128)} copy(f32[16,32,128]{2,1,0:T(8,128)S(1)} %get-tuple-element.5) | data formatting | bytes 524288
Async XLA Ops:
  0.6 1.0 %copy-start = (f32[16,32,128]{2,1,0:T(8,128)S(1)}, f32[16,32,128]{2,1,0:T(8,128)}, u32[]{:S(2)}) copy-start(f32[16,32,128]{2,1,0:T(8,128)} %rhs_ref.1) | copy-start | bytes 786436
  1.6 0.9 %copy-start.1 = (f32[16,32,128]{2,1,0:T(8,128)S(1)}, f32[16,32,128]{2,1,0:T(8,128)}, u32[]{:S(2)}) copy-start(f32[16,32,128]{2,1,0:T(8,128)} %scr_ref.1) | copy-start | bytes 786436
  2.5 0.7 copy-start.2

commit v2 on v1

v2 whole, which is shorter than its diff:
```python
import functools

import jax
import jax.numpy as jnp
from jax import lax
from jax.experimental import pallas as pl
from jax.experimental.pallas import tpu as pltpu
from jax.sharding import PartitionSpec as P

MESH = pl.DeviceIdType.MESH
F32 = jnp.float32
BF16 = jnp.bfloat16

NTX, NTY = 8, 16
HALO = 11
ROWS = 56
TOP = 12
PLANE = ROWS * 16
PITCH = 24
R1 = 32
DIRS8 = [(-1, -1), (1, -1), (-1, 1), (1, 1), (0, -1), (0, 1), (-1, 0), (1, 0)]
DIRS14 = [(-2, -1), (2, -1), (-2, 1), (2, 1)] + DIRS8[:6] + [(-2, 0), (2, 0), (-1, 0), (1, 0)]


def iota(shape, axis):
    return lax.broadcasted_iota(jnp.int32, shape, axis)


def dot_split(x, table):
    high = x.astype(BF16)
    low = (x - high.astype(F32)).astype(BF16)
    return jnp.dot(high, table, preferred_element_type=F32) + jnp.dot(
        low, table, preferred_element_type=F32
    )


def dot_exact(x, table):
    high = x.astype(BF16)
    rest = x - high.astype(F32)
    middle = rest.astype(BF16)
    low = (rest - middle.astype(F32)).astype(BF16)
    dot = functools.partial(jnp.dot, preferred_element_type=F32)
    return dot(high, table) + (dot(middle, table) + dot(low, table))


def kernel(
    rhs_hbm, scr_hbm, own_hbm, sol_ref, res_ref,
    rhs_ref, scr_ref, own_ref, s_in,
    bs1, b2, gain, va, vb, vc, q1, pk1, pk2, rp1, rp2, sl1, sl2, rs1, rs2, ebuf, xbuf, natural,
    l1s, l1g, l1b, l1x, l1v, l1w, l1e,
    m1ud, m1lr, m2ud, m2lr, rt1, rt2,
    l2b, l2s, l2g, l2v, l2w, l2e, l2x, l3g, l3m,
    split, merge, t12, u2, t23, p32, p21,
    arbuf, arr1, arr2,
    s_r1, r_r1, s_r2, r_r2, s_ar, r_ar,
):
    tx = lax.axis_index("tx")
    ty = lax.axis_index("ty")
    zero = lax.div(tx, 64)
    barrier = pltpu.get_barrier_semaphore()
    loads = [
        pltpu.make_async_copy(rhs_hbm, rhs_ref, s_in.at[0]),
        pltpu.make_async_copy(scr_hbm, scr_ref, s_in.at[1]),
        pltpu.make_async_copy(own_hbm, own_ref, s_in.at[2]),
    ]
    for load in loads:
        load.start()

    def inside(dx, dy):
        a, b = tx + dx, ty + dy
        return (a >= 0) & (a < NTX) & (b >= 0) & (b < NTY)

    def at(dx, dy):
        return {"tx": tx + dx, "ty": ty + dy}

    def ring(dx, dy):
        return {"tx": lax.rem(tx + dx, NTX), "ty": lax.rem(ty + dy, NTY)}

    ring_dirs = [(k, 0) for k in range(1, NTX)] + [(0, k) for k in range(1, NTY)]
    extra = [d for d in DIRS14 if d[0] != 0 and d[1] != 0]
    expected = jnp.int32(len(ring_dirs))
    for d in ring_dirs:
        pl.semaphore_signal(barrier, inc=1, device_id=ring(*d), device_id_type=MESH)
    for d in extra:
        ok = inside(*d)
        expected = expected + ok.astype(jnp.int32)

        @pl.when(ok)
        def _():
            pl.semaphore_signal(barrier, inc=1, device_id=at(*d), device_id_type=MESH)

    lane16 = iota((16, 128), 1)
    lane8 = iota((8, 128), 1)
    sub8 = iota((8, 128), 0)
    grp8 = lane8 >> 4
    half16 = lane16 >> 3
    own16 = (lane16 >= 32) & (lane16 < 96)
    own8 = (lane8 >= 32) & (lane8 < 96)
    side16 = ((lane16 >= 24) & (lane16 < 32)) | ((lane16 >= 96) & (lane16 < 104))
    side8 = ((lane8 >= 16) & (lane8 < 32)) | ((lane8 >= 96) & (lane8 < 112))
    z16 = jnp.zeros((16, 128), F32)
    z8 = jnp.zeros((8, 128), F32)

    def vrow(t, r):
        return pl.multiple_of(8 + (t * ROWS + r) * PITCH, 8)

    def brow(t, r):
        return pl.multiple_of((t * ROWS + r) * 16, 16)

    def stage(name, fn):
        fn()

    def take_inputs():
        for a, ref in enumerate((rhs_ref, scr_ref)):
            for i in range(2):
                x = [ref[pl.ds(16 * i + k, 16, stride=32), :] for k in range(16)]
                x = dot_exact(jnp.concatenate(x, axis=0), split[...])
                for t in (0, 1):
                    at_row = (t * ROWS + TOP + 16 * i) * 16
                    bs1[a, pl.ds(at_row, 256), :] = x[:, 128 * t : 128 * t + 128]

    def pack0(src, count, pk, sl):
        def body(j, c):
            span = pl.ds(pl.multiple_of(j * 16, 16), 16)
            for a in range(count):
                left, right = z16, z16
                for g in range(8):
                    even = src[a, pl.ds(brow(0, TOP + j * 8 + g), 16), :]
                    odd = src[a, pl.ds(brow(1, TOP + j * 8 + g), 16), :]
                    even = pltpu.roll(even, (16 * g - 88) % 128, 1)
                    odd = pltpu.roll(odd, (16 * g - 80) % 128, 1)
                    right = jnp.where(half16 == 2 * g, even, jnp.where(half16 == 2 * g + 1, odd, right))
                    left = jnp.where(
                        half16 == (2 * g - 7) % 16, even,
                        jnp.where(half16 == (2 * g - 6) % 16, odd, left),
                    )
                pk[0, a, span, :] = left
                pk[1, a, span, :] = right
            return c

        lax.fori_loop(0, 4, body, 0)
        for a in range(count):
            for m, first in ((0, TOP), (1, TOP + 32 - HALO)):
                for k in range(HALO):
                    even = src[a, pl.ds(brow(0, first + k), 16), :]
                    odd = src[a, pl.ds(brow(1, first + k), 16), :]
                    sl[m, a, pl.ds(16 * k, 16), :] = jnp.where(own16, even, pltpu.roll(odd, 64, 1))

    def unpack0(dst, count, rp, rs, x):
        def row(dxi, j, g):
            r = TOP + (dxi - 1) * 32 + j * 8 + g
            span = pl.ds(pl.multiple_of(j * 16, 16), 16)
            out = []
            for a in range(count):
                fl, fr = rp[dxi, 0, a, span, :], rp[dxi, 1, a, span, :]
                if dxi == 1:
                    even, odd = dst[a, pl.ds(brow(0, r), 16), :], dst[a, pl.ds(brow(1, r), 16), :]
                else:
                    k = j * 8 + g - (32 - HALO if dxi == 0 else 0)
                    both = rs[dxi // 2, a, pl.ds(16 * k, 16), :]
                    even, odd = jnp.where(own16, both, 0.0), jnp.where(own16, pltpu.roll(both, 64, 1), 0.0)
                ve = pltpu.roll(jnp.where(half16 == 2 * g, fl, fr), (24 - 16 * g) % 128, 1)
                vo = pltpu.roll(jnp.where(half16 == 2 * g + 1, fl, fr), (16 - 16 * g) % 128, 1)
                even, odd = jnp.where(side16, ve, even), jnp.where(side16, vo, odd)
                dst[a, pl.ds(brow(0, r), 16), :] = even
                dst[a, pl.ds(brow(1, r), 16), :] = odd
                out.append((even, odd))
            for t in (0, 1):
                at_row = pl.ds(brow(t, r), 16)
                if count == 2:
                    s = out[1][t]
                    gv = jnp.where(s > 0.0, 0.8 / (s + 6.0), 0.0)
                    gain[at_row, :] = gv
                else:
                    gv = gain[at_row, :]
                x[pl.ds(vrow(t, r), 16), :] = gv * out[0][t]

        def body(j, c):
            for g in range(8):
                row(1, j, g)
            return c

        lax.fori_loop(0, 4, body, 0)
        for j, groups in ((2, range(5, 8)), (3, range(8))):
            for g in groups:
                row(0, j, g)
        for j, groups in ((0, range(8)), (1, range(3))):
            for g in groups:
                row(2, j, g)

    def r1_copy(i, d, pk, rp, sl, rs, cyc):
        dx, dy = d
        if dy == 0:
            s, t = sl.at[0 if dx == -1 else 1], rs.at[1 if dx == -1 else 0]
        else:
            side = 0 if dy == -1 else 1
            if dx == 0:
                s, t = pk.at[side], rp.at[1, 1 - side]
            elif dx == -1:
                s, t = pk.at[side, :, pl.ds(0, 32)], rp.at[2, 1 - side, :, pl.ds(0, 32)]
            else:
                s, t = pk.at[side, :, pl.ds(32, 32)], rp.at[0, 1 - side, :, pl.ds(32, 32)]
        return pltpu.make_async_remote_copy(
            src_ref=s, dst_ref=t, send_sem=s_r1.at[cyc, i], recv_sem=r_r1.at[cyc, i],
            device_id=at(*d), device_id_type=MESH,
        )

    def start_r1(pk, rp, sl, rs, cyc):
        for i, d in enumerate(DIRS8):
            @pl.when(inside(*d))
            def _():
                r1_copy(i, d, pk, rp, sl, rs, cyc).start()

    def wait_r1(pk, rp, sl, rs, cyc):
        for i, d in enumerate(DIRS8):
            @pl.when(inside(-d[0], -d[1]))
            def _():
                r1_copy(i, d, pk, rp, sl, rs, cyc).wait_recv()

    def sent_r1(pk, rp, sl, rs, cyc):
        for i, d in enumerate(DIRS8):
            @pl.when(inside(*d))
            def _():
                r1_copy(i, d, pk, rp, sl, rs, cyc).wait_send()

    def clear_r1(src, count, rp, rs):
        for a in range(count):
            for t in (0, 1):
                for r in (0, ROWS - 1):
                    src[a, pl.ds(brow(t, r), 16), :] = z16
        for i, dx in ((0, -1), (1, 1)):
            @pl.when(jnp.logical_not(inside(dx, 0)))
            def _():
                rs[i] = jnp.zeros((count, HALO * 16, 128), F32)
        for dxi in range(3):
            for sidei, dy in ((0, -1), (1, 1)):
                @pl.when(jnp.logical_not(inside(dxi - 1, dy)))
                def _():
                    rp[dxi, sidei] = jnp.zeros((count, 64, 128), F32)

    def r2_copy(i, d, mud, mlr, rt, cyc):
        dx, dy = d
        ns = 2 - cyc
        if dy == 0:
            n = (6 + ns - cyc) if abs(dx) == 1 else ns
            s = mud.at[0 if dx < 0 else 1, pl.ds(0, n)]
        else:
            n = (2 + ns) if abs(dx) <= 1 else ns
            s = mlr.at[0 if dy < 0 else 1, pl.ds(0, n)]
        return pltpu.make_async_remote_copy(
            src_ref=s, dst_ref=rt.at[2 - dx, 1 - dy, pl.ds(0, n)],
            send_sem=s_r2.at[cyc, i], recv_sem=r_r2.at[cyc, i],
            device_id=at(*d), device_id_type=MESH,
        )

    def each_r2(op, mud, mlr, rt, cyc):
        for i, d in enumerate(DIRS14):
            @pl.when(inside(-d[0], -d[1]) if op == "wait_recv" else inside(*d))
            def _():
                getattr(r2_copy(i, d, mud, mlr, rt, cyc), op)()

    def clear_r2(rt):
        for dx, dy in DIRS14:
            @pl.when(jnp.logical_not(inside(dx, dy)))
            def _():
                rt[2 + dx, 1 + dy] = jnp.zeros((8, 8, 128), F32)

    def ar_copy(cyc, i):
        if i < 7:
            d, s, t = ring(i + 1, 0), arbuf.at[cyc, 0], arr1.at[cyc, i]
        else:
            d, s, t = ring(0, i - 6), arbuf.at[cyc, 1], arr2.at[cyc, i - 7]
        return pltpu.make_async_remote_copy(
            src_ref=s, dst_ref=t, send_sem=s_ar.at[cyc, i], recv_sem=r_ar.at[cyc, i],
            device_id=d, device_id_type=MESH,
        )

    def ar_begin(cyc, rows):
        out = jnp.zeros((1, 128), F32)
        for k, acc in enumerate(rows):
            acc = jnp.sum(jnp.where(own8, acc, 0.0), axis=0, keepdims=True)
            out = jnp.where(lane8[:1] == k, jnp.sum(acc, axis=1, keepdims=True), out)
        arbuf[cyc, 0] = out
        for i in range(7):
            ar_copy(cyc, i).start()

    def ar_middle(cyc):
        total = arbuf[cyc, 0]
        for i in range(7):
            ar_copy(cyc, i).wait_recv()
        for i in range(7):
            total = total + arr1[cyc, i]
        arbuf[cyc, 1] = total
        for i in range(7, 22):
            ar_copy(cyc, i).start()

    def ar_end(cyc, count):
        total = arbuf[cyc, 1]
        for i in range(7, 22):
            ar_copy(cyc, i).wait_recv()
        for i in range(15):
            total = total + arr2[cyc, i]
        return [jnp.broadcast_to(total[:, k : k + 1], (8, 128)) for k in range(count)]

    def stencil0(src, r, count, put):
        rows = [
            [src[pl.ds(vrow(t, r + k - 1), 16), :] for k in range(count + 2)] for t in (0, 1)
        ]
        for k in range(count):
            even, odd = rows[0][k + 1], rows[1][k + 1]
            beside = (odd + pltpu.roll(odd, 1, 1), even + pltpu.roll(even, 127, 1))
            for t in (0, 1):
                at_row = vrow(t, r + k)
                n = rows[t][k] + rows[t][k + 2]
                n = n + (src[pl.ds(at_row - 1, 16), :] + src[pl.ds(at_row + 1, 16), :])
                put(k, t, rows[t][k + 1], n + beside[t])

    def sweep0(src, dst, bref, r0, count, per):
        def body(i, carry):
            r = r0 + per * i

            def put(k, t, c, n):
                row = pl.ds(brow(t, r + k), 16)
                dst[pl.ds(vrow(t, r + k), 16), :] = 0.2 * c + gain[row, :] * (bref[0, row, :] + n)

            stencil0(src, r, per, put)
            return carry

        lax.fori_loop(0, count // per, body, 0)

    def restrict0(out):
        x = ebuf[pl.ds(0, 192, stride=2), :] + ebuf[pl.ds(1, 192, stride=2), :]
        out[pl.ds(32, 192), :] = 0.125 * x

    def wrow(r):
        return pl.multiple_of(8 + r * 16, 8)

    def stencil1(src, r, count, put):
        rows = [src[pl.ds(wrow(r + k - 1), 8), :] for k in range(count + 2)]
        for k in range(count):
            c = rows[k + 1]
            n = rows[k] + rows[k + 2]
            n = n + (src[pl.ds(wrow(r + k) - 1, 8), :] + src[pl.ds(wrow(r + k) + 1, 8), :])
            n = n + (pltpu.roll(c, 1, 1) + pltpu.roll(c, 127, 1))
            put(k, c, n)

    def sweep1(src, dst):
        def put(k, c, n):
            row = pl.ds((4 + k) * 8, 8)
            dst[pl.ds(wrow(4 + k + zero), 8), :] = 0.2 * c + l1g[row, :] * (l1b[row, :] + 0.5 * n)

        stencil1(src, 4 + zero, 24, put)

    def restrict1():
        parts = []
        for z in range(4):
            x = l1e[pl.ds(2 * z, 8, stride=16), :] + l1e[pl.ds(2 * z + 1, 8, stride=16), :]
            x = x + l1e[pl.ds(2 * z + 8, 8, stride=16), :] + l1e[pl.ds(2 * z + 9, 8, stride=16), :]
            parts.append(x)
        return dot_split(jnp.concatenate(parts, axis=1), t12[...])

    def base2(z, k):
        return z * 56 + 8 + 8 * k + zero

    def stencil2(src, z, k):
        c = src[pl.ds(base2(z, k), 8), :]
        n = src[pl.ds(base2(z, k) - 1, 8), :] + src[pl.ds(base2(z, k) + 1, 8), :]
        if z > 0:
            n = n + src[pl.ds(base2(z - 1, k), 8), :]
        if z < 3:
            n = n + src[pl.ds(base2(z + 1, k), 8), :]
        return c, n + (pltpu.roll(c, 1, 1) + pltpu.roll(c, 127, 1))

    def sweep2(src, dst, tiles):
        for z in range(4):
            for k in tiles:
                c, n = stencil2(src, z, k)
                row = pl.ds(z * 40 + 8 * k, 8)
                dst[pl.ds(base2(z, k), 8), :] = 0.2 * c + l2g[row, :] * (l2b[row, :] + 0.25 * n)

    def table(ref, rows, cols, value, f):
        ref[...] = jnp.where(f(iota((rows, cols), 0), iota((rows, cols), 1)), value, 0.0).astype(BF16)

    def prepare():
        tables()
        zeros()

    def tables():
        table(merge, 256, 128, 1.0, lambda i, o: ((i & 127) - 32 == o >> 1) & ((i >> 7) == (o & 1)))
        table(t12, 512, 128, 0.125, lambda i, o: (((i & 127) - 32) >> 1 == (o & 31)) & ((i >> 7) == (o >> 5)))
        table(t23, 128, 128, 0.125, lambda i, o: ((i - 48) >> 1) == o - 56)
        table(u2, 384, 512, 1.0, lambda i, o: (((i & 127) >> 5) == (o >> 7)) & ((o & 127) - 48 == ((i >> 7) - 1) * 32 + (i & 31)))
        table(p32, 128, 128, 1.0, lambda i, o: ((o - 48) >> 1) == i - 56)
        table(p21, 128, 128, 1.0, lambda i, o: ((o - 32) >> 1) == i - 48)

    def zeros():
        def clear_pads(i, c):
            for ref in (va, vb, vc):
                ref[pl.ds(pl.multiple_of(i * PITCH, 8), 8), :] = z8
            return c

        lax.fori_loop(0, 2 * ROWS + 1, clear_pads, 0)
        for ref in (vb, vc):
            for t in (0, 1):
                for r in (0, 1, ROWS - 2, ROWS - 1):
                    ref[pl.ds(vrow(t, r), 16), :] = z16
        for ref in (l1v, l1w):
            ref[...] = jnp.zeros(ref.shape, F32)
        for ref in (l1s, l1g, l1b):
            ref[...] = jnp.zeros(ref.shape, F32)
        for ref in (l2v, l2w):
            ref[...] = jnp.zeros(ref.shape, F32)
        clear_r1(bs1, 2, rp1, rs1)
        clear_r1(b2, 1, rp2, rs2)
        clear_r2(rt1)
        clear_r2(rt2)

    table(split, 128, 256, 1.0, lambda i, o: ((o & 127) - 32 == i >> 1) & ((o >> 7) == (i & 1)))
    for load in loads:
        load.wait()
    stage("take_inputs", take_inputs)
    here = own_ref[0, ty]
    link_l = jnp.where(own_ref[0, jnp.maximum(ty - 1, 0)] == here, 1.0, 0.0)
    link_r = jnp.where(own_ref[0, jnp.minimum(ty + 1, NTY - 1)] == here, 1.0, 0.0)
    link = jnp.where(lane8 == 56, link_l, jnp.where(lane8 == 72, link_r, 1.0))

    def screen_sums(first, count):
        for i in range(first, first + count):
            even = bs1[1, pl.ds(brow(0, 4 + 2 * i), 32), :]
            odd = bs1[1, pl.ds(brow(1, 4 + 2 * i), 32), :]
            x = even + odd
            ebuf[pl.ds(i * 16, 16), :] = x[:16] + x[16:]

    def own_screens():
        screen_sums(4, 16)
        x = ebuf[pl.ds(64, 128, stride=2), :] + ebuf[pl.ds(65, 128, stride=2), :]
        l1e[...] = 0.125 * x
        s2_own = restrict1()
        for m in (0, 1):
            m1ud[m, 1] = s2_own
            m1lr[m, 1] = s2_own
            m1ud[m, 7] = link
        rt1[2, 1, 1] = s2_own

    def vcycle(cyc, src, pk, rp, sl, rs, mud, mlr, rt, x, y):
        ns = 2 - cyc

        def screens1():
            screen_sums(0, 24)
            restrict0(l1s)
            s = l1s[...]
            l1g[...] = jnp.where(s > 0.0, 0.8 / (s + 3.0), 0.0)

        def defect0():
            per = 24

            def body(i, c):
                r = 4 + per * i
                held = []

                def put(k, t, centre, n):
                    row = pl.ds(brow(t, r + k), 16)
                    held.append(src[0, row, :] - (bs1[1, row, :] + 6.0) * centre + n)
                    if len(held) == 4:
                        at_row = pl.multiple_of((i * (per // 2) + k // 2) * 16, 16)
                        ebuf[pl.ds(at_row, 16), :] = (held[0] + held[1]) + (held[2] + held[3])
                        held.clear()

                stencil0(x, r, per, put)
                return c

            lax.fori_loop(0, 48 // per, body, 0)

        def start1():
            for r in range(4, 28):
                row = pl.ds(r * 8, 8)
                l1v[pl.ds(wrow(r), 8), :] = l1g[row, :] * l1b[row, :]

        def defect1():
            def put(k, centre, n):
                row = pl.ds((8 + k) * 8, 8)
                l1e[pl.ds(k * 8, 8), :] = l1b[row, :] - (l1s[row, :] + 3.0) * centre + 0.5 * n

            stencil1(l1v, 8 + zero, 16, put)

        def pack1():
            for m in (0, 1):
                for k in range(5):
                    mud[m, ns + k] = l1v[pl.ds(wrow(8 + k + 11 * m), 8), :]
            for j in (0, 1):
                left, right = z8, z8
                for g in range(8):
                    v = pltpu.roll(l1v[pl.ds(wrow(8 + 8 * j + g), 8), :], (16 * g - 80) % 128, 1)
                    right = jnp.where(grp8 == g, v, right)
                    left = jnp.where(grp8 == (g + 5) % 8, v, left)
                mlr[0, ns + j] = left
                mlr[1, ns + j] = right

        def down1():
            b2_own = restrict1()
            for m in (0, 1):
                mud[m, 0] = b2_own
                mlr[m, 0] = b2_own
            rt[2, 1, 0] = b2_own

        def unpack2():
            for a in range(ns):
                block = jnp.concatenate(
                    [
                        jnp.concatenate([rt[dxi, dyi, a] for dxi in range(5)], axis=0)
                        for dyi in range(3)
                    ],
                    axis=1,
                )
                spread = dot_split(block, u2[...])
                for z in range(4):
                    part = spread[:, 128 * z : 128 * z + 128]
                    if a == 0:
                        l2b[pl.ds(z * 40, 40), :] = part
                    else:
                        l2s[pl.ds(z * 40, 40), :] = part

        def screens3():
            s = l2s[...]
            l2g[...] = jnp.where(s > 0.0, 0.8 / (s + 1.5), 0.0)
            for z in range(2):
                l2e[pl.ds(z * 40, 40), :] = (
                    l2s[pl.ds(2 * z * 40, 40), :] + l2s[pl.ds((2 * z + 1) * 40, 40), :]
                )
            s = restrict2()
            l3g[...] = jnp.where(s > 0.0, 0.8 / (s + 0.75), 0.0)
            up, down = rt[1, 1, 7], rt[3, 1, 7]
            for k, m in enumerate((jnp.where(sub8 < 4, up, link), down)):
                l3m[0, k] = 0.125 * m
                l3m[1, k] = pltpu.roll(0.125 * m, 127, 1)

        def down2():
            for z in range(4):
                for k in range(5):
                    row = pl.ds(z * 40 + 8 * k, 8)
                    l2v[pl.ds(base2(z, k), 8), :] = l2g[row, :] * l2b[row, :]
            sweep2(l2v, l2w, range(5))
            sweep2(l2w, l2v, range(5))
            for k in range(5):
                d = []
                for z in range(4):
                    c, n = stencil2(l2v, z, k)
                    row = pl.ds(z * 40 + 8 * k, 8)
                    d.append(l2b[row, :] - (l2s[row, :] + 1.5) * c + 0.25 * n)
                l2e[pl.ds(8 * k, 8), :] = d[0] + d[1]
                l2e[pl.ds(40 + 8 * k, 8), :] = d[2] + d[3]

        def up2():
            for z in range(4):
                for k in (1, 2, 3):
                    row = pl.ds(base2(z, k), 8)
                    l2v[row, :] = l2v[row, :] + l2x[pl.ds((z // 2) * 32 + 8 * (k - 1), 8), :]
            sweep2(l2v, l2w, (1, 2, 3))
            sweep2(l2w, l2v, (1, 2, 3))
            sweep2(l2v, l2w, (1, 2, 3))
            e2 = jnp.concatenate([l2w[pl.ds(z * 56 + 20 + zero, 16), :] for z in range(4)], axis=0)
            e2 = dot_split(e2, p21[...])
            for z in range(4):
                for a in (0, 8):
                    for b in (0, 1):
                        l1x[pl.ds(a + 2 * z + b, 16, stride=16), :] = e2[16 * z : 16 * z + 16]

        def correct1():
            for r in range(3, 29):
                tile, inner = (r - 8) // 16, (r - 8) % 16
                j, g = inner // 8, inner % 8
                v = jnp.where(grp8 == g, rt[2 + tile, 0, ns + j], rt[2 + tile, 2, ns + j])
                v = pltpu.roll(v, (16 - 16 * g) % 128, 1)
                if tile == 0:
                    base = l1v[pl.ds(wrow(r), 8), :]
                elif tile < 0:
                    base = rt[1, 1, ns + inner - 11]
                else:
                    base = rt[3, 1, ns + inner]
                l1v[pl.ds(wrow(r), 8), :] = jnp.where(side8, v, base) + l1x[pl.ds(r * 8, 8), :]

        def up1():
            e1 = jnp.concatenate([l1w[pl.ds(wrow(6 + k), 8), :] for k in range(20)], axis=0)
            for b in (0, 1):
                xbuf[pl.ds(b, 160, stride=2), :] = e1

        def correct0():
            def body(i, c):
                e = xbuf[pl.ds(pl.multiple_of(i * 16, 16), 16), :]
                for t in (0, 1):
                    for k in (0, 1):
                        row = pl.ds(vrow(t, 8 + 2 * i + k), 16)
                        x[row, :] = x[row, :] + e
                return c

            lax.fori_loop(0, 20, body, 0, unroll=10)

        wait_r1(pk, rp, sl, rs, cyc)
        stage("unpack0", lambda: unpack0(src, ns, rp, rs, x))
        if cyc == 0:
            stage("screens1", screens1)
        stage("sweep0pre", lambda: sweep0(x, y, src, 2, 52, 26))
        sweep0(y, x, src, 2, 52, 26)
        stage("defect0", defect0)
        stage("restrict0", lambda: restrict0(l1b))
        stage("start1", start1)
        stage("sweep1", lambda: sweep1(l1v, l1w))
        sweep1(l1w, l1v)
        stage("pack1", pack1)
        stage("defect1", defect1)
        stage("down1", down1)
        each_r2("start", mud, mlr, rt, cyc)
        each_r2("wait_recv", mud, mlr, rt, cyc)
        stage("unpack2", unpack2)
        if cyc == 0:
            stage("screens3", screens3)
        stage("down2", down2)
        stage("solve3", lambda: solve3(restrict2()))
        stage("up2", up2)
        stage("correct1", correct1)
        sweep1(l1v, l1w)
        sweep1(l1w, l1v)
        sweep1(l1v, l1w)
        stage("up1", up1)
        stage("correct0", correct0)
        stage("sweep0post", lambda: sweep0(x, y, src, 8, 40, 20))
        sweep0(y, x, src, 10, 36, 18)
        sweep0(x, y, src, 10, 36, 18)

    def restrict2():
        parts = [
            l2e[pl.ds(z * 40 + 8, 16, stride=2), :] + l2e[pl.ds(z * 40 + 9, 16, stride=2), :]
            for z in range(2)
        ]
        return dot_split(jnp.concatenate(parts, axis=0), t23[...])

    def solve3(b3):
        up_ok = jnp.where((sub8 & 3) != 0, 0.125, 0.0)
        down_ok = jnp.where((sub8 & 3) != 3, 0.125, 0.0)
        g = [[l3g[pl.ds(16 * z + 8 * k, 8), :] for k in (0, 1)] for z in (0, 1)]
        b = [[b3[16 * z + 8 * k : 16 * z + 8 * k + 8] for k in (0, 1)] for z in (0, 1)]
        ml, mr = [l3m[0, 0], l3m[0, 1]], [l3m[1, 0], l3m[1, 1]]
        v = [[g[z][k] * b[z][k] for k in (0, 1)] for z in (0, 1)]
        for counter in range(7):
            new = [[None, None], [None, None]]
            for z in (0, 1):
                for k in (0, 1):
                    c = v[z][k]
                    n = 0.125 * v[1 - z][k]
                    n = n + pltpu.roll(c, 1, 0) * up_ok + pltpu.roll(c, 7, 0) * down_ok
                    n = n + pltpu.roll(c, 1, 1) * ml[k] + pltpu.roll(c, 127, 1) * mr[k]
                    new[z][k] = 0.2 * c + g[z][k] * (b[z][k] + n)
            v = new
        e3 = jnp.concatenate([v[0][0], v[0][1], v[1][0], v[1][1]], axis=0)
        e3 = dot_split(e3, p32[...])
        for z in (0, 1):
            for a in (0, 1):
                l2x[pl.ds(z * 32 + a, 16, stride=2), :] = e3[16 * z : 16 * z + 16]

    stage("pack0x2", lambda: pack0(bs1, 2, pk1, sl1))
    pl.semaphore_wait(barrier, expected)
    start_r1(pk1, rp1, sl1, rs1, 0)
    stage("prepare", prepare)
    stage("own_screens", own_screens)

    vcycle(0, bs1, pk1, rp1, sl1, rs1, m1ud, m1lr, rt1, va, vb)

    def halves(a):
        return a[0:8] + a[8:16]

    def apply_first(i, acc):
        r = TOP + 16 * i
        acc = list(acc)

        def put(k, t, c, n):
            row = pl.ds(brow(t, r + k), 16)
            q = (bs1[1, row, :] + 6.0) * c - n
            b2[0, row, :] = q
            acc[0] = acc[0] + halves(bs1[0, row, :] * c)
            acc[1] = acc[1] + halves(c * q)

        stencil0(vb, r, 16, put)
        return tuple(acc)

    sums = lax.fori_loop(0, 2, apply_first, (z8, z8))
    stage("pack0x1", lambda: pack0(b2, 1, pk2, sl2))
    start_r1(pk2, rp2, sl2, rs2, 1)
    ar_begin(0, sums)
    ar_middle(0)

    vcycle(1, b2, pk2, rp2, sl2, rs2, m2ud, m2lr, rt2, va, vc)
    rho0, curv0 = ar_end(0, 2)
    step0 = rho0 / curv0
    step0_16 = jnp.concatenate([step0, step0], axis=0)

    def next_z(i, c):
        for k in (0, 1):
            for t in (0, 1):
                row = pl.ds(vrow(t, TOP - 2 + 2 * i + k), 16)
                vc[row, :] = vb[row, :] - step0_16 * vc[row, :]
        return c

    lax.fori_loop(0, 18, next_z, 0, unroll=9)

    def apply_second(i, acc):
        r = TOP + 16 * i
        acc = list(acc)

        def put(k, t, c, n):
            row = pl.ds(brow(t, r + k), 16)
            q = (bs1[1, row, :] + 6.0) * c - n
            q1[row, :] = q
            q0 = b2[0, row, :]
            z0 = vb[pl.ds(vrow(t, r + k), 16), :]
            acc[0] = acc[0] + halves((bs1[0, row, :] - step0_16 * q0) * c)
            acc[1] = acc[1] + halves(c * q)
            acc[2] = acc[2] + halves(c * q0 + z0 * q)

        stencil0(vc, r, 16, put)
        return tuple(acc)

    sums = lax.fori_loop(0, 2, apply_second, (z8, z8, z8))
    ar_begin(1, sums)
    ar_middle(1)
    rho1, zz, cross = ar_end(1, 3)
    beta = rho1 / rho0
    curv1 = zz + beta * (cross + beta * curv0)
    step1 = rho1 / curv1
    mixed = step0 + step1 * beta

    def finish():
        mixed_16 = jnp.concatenate([mixed, mixed], axis=0)
        step1_16 = jnp.concatenate([step1, step1], axis=0)

        def body(i, c):
            sol, app = [], []
            for k in range(8):
                r = TOP + 8 * i + k
                z, q = [], []
                for t in (0, 1):
                    v, b = pl.ds(vrow(t, r), 16), pl.ds(brow(t, r), 16)
                    z.append(mixed_16 * vb[v, :] + step1_16 * vc[v, :])
                    q.append(mixed_16 * b2[0, b, :] + step1_16 * q1[b, :])
                sol.append(jnp.concatenate(z, axis=1))
                app.append(jnp.concatenate(q, axis=1))
            for a, rows in ((0, sol), (1, app)):
                natural[a] = dot_exact(jnp.concatenate(rows, axis=0), merge[...])
            at_rows = pl.ds(pl.multiple_of(8 * i, 8), 8)
            for z in range(16):
                sol_ref[z, at_rows, :] = natural[0, pl.ds(z, 8, stride=16), :]
                res_ref[z, at_rows, :] = (
                    rhs_ref[pl.ds(pl.multiple_of(z * 32 + 8 * i, 8), 8), :]
                    - natural[1, pl.ds(z, 8, stride=16), :]
                )
            return c

        lax.fori_loop(0, 4, body, 0)

    stage("finish", finish)

    sent_r1(pk1, rp1, sl1, rs1, 0)
    sent_r1(pk2, rp2, sl2, rs2, 1)
    each_r2("wait_send", m1ud, m1lr, rt1, 0)
    each_r2("wait_send", m2ud, m2lr, rt2, 1)
    for cyc in (0, 1):
        for i in range(22):
            ar_copy(cyc, i).wait_send()


def on_device(right_side, screening, owners):
    vm = lambda *s: pltpu.VMEM(s, F32)
    bm = lambda *s: pltpu.VMEM(s, BF16)
    padded = 8 + 2 * ROWS * PITCH + 8
    scratch = [
        vm(512, 128), vm(512, 128), pltpu.SMEM(owners.shape, jnp.int32),
        pltpu.SemaphoreType.DMA((3,)),
        vm(2, 2 * PLANE, 128), vm(1, 2 * PLANE, 128), vm(2 * PLANE, 128),
        vm(padded, 128), vm(padded, 128), vm(padded, 128), vm(2 * PLANE, 128),
        vm(2, 2, 64, 128), vm(2, 1, 64, 128), vm(3, 2, 2, 64, 128), vm(3, 2, 1, 64, 128),
        vm(2, 2, HALO * 16, 128), vm(2, 1, HALO * 16, 128), vm(2, 2, HALO * 16, 128), vm(2, 1, HALO * 16, 128),
        vm(24 * 16, 128), vm(20 * 16, 128), vm(2, 128, 128),
        vm(R1 * 8, 128), vm(R1 * 8, 128), vm(R1 * 8, 128), vm(R1 * 8, 128),
        vm(R1 * 16 + 16, 128), vm(R1 * 16 + 16, 128), vm(128, 128),
        vm(2, 8, 8, 128), vm(2, 4, 8, 128), vm(2, 8, 8, 128), vm(2, 4, 8, 128),
        vm(5, 3, 8, 8, 128), vm(5, 3, 8, 8, 128),
        vm(160, 128), vm(160, 128), vm(160, 128), vm(4 * 56, 128), vm(4 * 56, 128),
        vm(80, 128), vm(64, 128), vm(32, 128), vm(2, 2, 8, 128),
        bm(128, 256), bm(256, 128), bm(512, 128), bm(384, 512), bm(128, 128), bm(128, 128), bm(128, 128),
        vm(2, 2, 1, 128), vm(2, 7, 1, 128), vm(2, 15, 1, 128),
        pltpu.SemaphoreType.DMA((2, 8)), pltpu.SemaphoreType.DMA((2, 8)),
        pltpu.SemaphoreType.DMA((2, 14)), pltpu.SemaphoreType.DMA((2, 14)),
        pltpu.SemaphoreType.DMA((2, 22)), pltpu.SemaphoreType.DMA((2, 22)),
    ]
    block = jax.ShapeDtypeStruct(right_side.shape, F32)
    vmem = pl.BlockSpec(memory_space=pltpu.VMEM)
    return tuple(
        pl.pallas_call(
            kernel,
            out_shape=(block, block),
            in_specs=[pl.BlockSpec(memory_space=pl.ANY)] * 3,
            out_specs=(vmem, vmem),
            scratch_shapes=scratch,
            compiler_params=pltpu.CompilerParams(
                collective_id=0, has_side_effects=True, vmem_limit_bytes=60 * 2**20
            ),
        )(right_side.reshape(512, 128), screening.reshape(512, 128), owners)
    )


def solution(mesh):
    spec = P(None, "tx", "ty")
    return jax.shard_map(
        on_device, mesh=mesh, in_specs=(spec, spec, P("tx", None)), out_specs=(spec, spec),
        check_vma=False,
    )
```

time: 69.2 us -> 55.1 us (0.80)
  Pallas kernels: 64.1 us -> 51.9 us
  local copies, waits for them, and re-layouts: 3.95 us -> 2.42 us
    pallas_call x1, Pallas kernels: 64.1 us -> 51.9 us  [on_device(): pl.pallas_call(kernel, out_shape=(block, block), in_specs=[pl.BlockSpec(m...]
    unnamed x8 -> x4, local copies, waits for them, and re-layouts: 3.95 us -> 2.42 us
where the time goes in v2:
time: 55.1 us; the launch traced here: 54.9 us
  Pallas kernels  51.9 us (94%)
  local copies, waits for them, and re-layouts  2.42 us (4%)
  between operations  0.65 us (1%)
    pallas_call x1, Pallas kernels, on_device(): pl.pallas_call(kernel, out_shape=(block, block), in_specs=[pl.BlockSpec(m...  51.9 us
    unnamed x4, local copies, waits for them, and re-layouts  2.42 us

profile of v2, /device:TPU:0, one launch (start us, length us, event | category | flops | bytes accessed | tf_op | source)
XLA Modules:
  0.0 54.9 jit_solution(12394867559657310476)
XLA Ops:
  0.6 51.9 %shard_map.50 = (f32[16,32,128]{2,1,0:T(8,128)}, f32[16,32,128]{2,1,0:T(8,128)}) custom-call(f32[512,128]{1,0:T(8,128)} %bitcast.2, f32[512,128]{1,0:T(8,128)} %bitcast.3, s32[1,16]{1,0:T(1,128)} %own_hbm.1), custom_call_target="tpu_custom_call" | custom-call | tf_op jit(solution)/shard_map/pallas_call | solution.py:797
  52.5 0.0 copy-start
  52.5 1.7 %copy.7 = f32[16,32,128]{2,1,0:T(8,128)} copy(f32[16,32,128]{2,1,0:T(8,128)} %get-tuple-element.4) | data formatting | bytes 524288
  54.2 0.0 copy-done
  54.2 0.7 %copy.8 = f32[16,32,128]{2,1,0:T(8,128)} copy(f32[16,32,128]{2,1,0:T(8,128)S(1)} %copy-done) | data formatting | bytes 524288
Async XLA Ops:
  52.5 1.7 %copy-start = (f32[16,32,128]{2,1,0:T(8,128)S(1)}, f32[16,32,128]{2,1,0:T(8,128)}, u32[]{:S(2)}) copy-start(f32[16,32,128]{2,1,0:T(8,128)} %get-tuple-element.5) | copy-start | bytes 786436

commit v3 on v2

--- a/solution.py
+++ b/solution.py
@@ -27,20 +27,19 @@
 
 
 def dot_split(x, table):
-    high = x.astype(BF16)
-    low = (x - high.astype(F32)).astype(BF16)
-    return jnp.dot(high, table, preferred_element_type=F32) + jnp.dot(
-        low, table, preferred_element_type=F32
-    )
+    high = x.astype(BF16).astype(F32)
+    parts = jnp.concatenate([high, x - high], axis=0).astype(BF16)
+    out = jnp.dot(parts, table, preferred_element_type=F32)
+    return out[: x.shape[0]] + out[x.shape[0] :]
 
 
 def dot_exact(x, table):
-    high = x.astype(BF16)
-    rest = x - high.astype(F32)
-    middle = rest.astype(BF16)
-    low = (rest - middle.astype(F32)).astype(BF16)
-    dot = functools.partial(jnp.dot, preferred_element_type=F32)
-    return dot(high, table) + (dot(middle, table) + dot(low, table))
+    high = x.astype(BF16).astype(F32)
+    middle = (x - high).astype(BF16).astype(F32)
+    parts = jnp.concatenate([high, middle, x - high - middle], axis=0).astype(BF16)
+    out = jnp.dot(parts, table, preferred_element_type=F32)
+    n = x.shape[0]
+    return out[:n] + (out[n : 2 * n] + out[2 * n :])
 
 
 def kernel(
@@ -48,9 +47,9 @@
     rhs_ref, scr_ref, own_ref, s_in,
     bs1, b2, gain, va, vb, vc, q1, pk1, pk2, rp1, rp2, sl1, sl2, rs1, rs2, ebuf, xbuf, natural,
     l1s, l1g, l1b, l1x, l1v, l1w, l1e,
-    m1ud, m1lr, m2ud, m2lr, rt1, rt2,
+    tb1, tb2, sd1, sd2, st1, st2, rt1, rt2, rd1, rd2, rx1, rx2,
     l2b, l2s, l2g, l2v, l2w, l2e, l2x, l3g, l3m,
-    split, merge, t12, u2, t23, p32, p21,
+    split, merge, t12, t23, p32, p21,
     arbuf, arr1, arr2,
     s_r1, r_r1, s_r2, r_r2, s_ar, r_ar,
 ):
@@ -93,6 +92,7 @@
     lane8 = iota((8, 128), 1)
     sub8 = iota((8, 128), 0)
     grp8 = lane8 >> 4
+    quarter = lane8 >> 5
     half16 = lane16 >> 3
     own16 = (lane16 >= 32) & (lane16 < 96)
     own8 = (lane8 >= 32) & (lane8 < 96)
@@ -120,7 +120,7 @@
                     bs1[a, pl.ds(at_row, 256), :] = x[:, 128 * t : 128 * t + 128]
 
     def pack0(src, count, pk, sl):
-        def body(j, c):
+        for j in range(4):
             span = pl.ds(pl.multiple_of(j * 16, 16), 16)
             for a in range(count):
                 left, right = z16, z16
@@ -136,9 +136,6 @@
                     )
                 pk[0, a, span, :] = left
                 pk[1, a, span, :] = right
-            return c
-
-        lax.fori_loop(0, 4, body, 0)
         for a in range(count):
             for m, first in ((0, TOP), (1, TOP + 32 - HALO)):
                 for k in range(HALO):
@@ -175,12 +172,9 @@
                     gv = gain[at_row, :]
                 x[pl.ds(vrow(t, r), 16), :] = gv * out[0][t]
 
-        def body(j, c):
+        for j in range(4):
             for g in range(8):
                 row(1, j, g)
-            return c
-
-        lax.fori_loop(0, 4, body, 0)
         for j, groups in ((2, range(5, 8)), (3, range(8))):
             for g in groups:
                 row(0, j, g)
@@ -238,32 +232,37 @@
                 def _():
                     rp[dxi, sidei] = jnp.zeros((count, 64, 128), F32)
 
-    def r2_copy(i, d, mud, mlr, rt, cyc):
+    def r2_copy(i, d, bufs, cyc):
+        tb, sd, st, rt, rd, rx = bufs
         dx, dy = d
-        ns = 2 - cyc
-        if dy == 0:
-            n = (6 + ns - cyc) if abs(dx) == 1 else ns
-            s = mud.at[0 if dx < 0 else 1, pl.ds(0, n)]
+        if i < 14:
+            s, t = tb.at[1 + dy], rt.at[2 - dx, 1 - dy]
+        elif dy == 0:
+            s, t = sd.at[0 if dx < 0 else 1], rd.at[1 if dx < 0 else 0]
         else:
-            n = (2 + ns) if abs(dx) <= 1 else ns
-            s = mlr.at[0 if dy < 0 else 1, pl.ds(0, n)]
+            side = 0 if dy < 0 else 1
+            s, t = st.at[side], rx.at[1 - dx, 1 - side]
         return pltpu.make_async_remote_copy(
-            src_ref=s, dst_ref=rt.at[2 - dx, 1 - dy, pl.ds(0, n)],
-            send_sem=s_r2.at[cyc, i], recv_sem=r_r2.at[cyc, i],
+            src_ref=s, dst_ref=t, send_sem=s_r2.at[cyc, i], recv_sem=r_r2.at[cyc, i],
             device_id=at(*d), device_id_type=MESH,
         )
 
-    def each_r2(op, mud, mlr, rt, cyc):
-        for i, d in enumerate(DIRS14):
+    def each_r2(op, part, bufs, cyc):
+        for i, d in enumerate(DIRS14) if part == 0 else enumerate(DIRS8, 14):
             @pl.when(inside(-d[0], -d[1]) if op == "wait_recv" else inside(*d))
             def _():
-                getattr(r2_copy(i, d, mud, mlr, rt, cyc), op)()
-
-    def clear_r2(rt):
+                getattr(r2_copy(i, d, bufs, cyc), op)()
+
+    def clear_r2(rt, rd, rx):
         for dx, dy in DIRS14:
             @pl.when(jnp.logical_not(inside(dx, dy)))
             def _():
-                rt[2 + dx, 1 + dy] = jnp.zeros((8, 8, 128), F32)
+                rt[2 + dx, 1 + dy] = jnp.zeros(rt.shape[2:], F32)
+                if abs(dx) <= 1:
+                    if dy == 0:
+                        rd[(dx + 1) // 2] = jnp.zeros(rd.shape[1:], F32)
+                    else:
+                        rx[1 + dx, (dy + 1) // 2] = jnp.zeros(rx.shape[2:], F32)
 
     def ar_copy(cyc, i):
         if i < 7:
@@ -293,6 +292,9 @@
         arbuf[cyc, 1] = total
         for i in range(7, 22):
             ar_copy(cyc, i).start()
+        if cyc == 1:
+            for i in range(7):
+                ar_copy(cyc, i).wait_send()
 
     def ar_end(cyc, count):
         total = arbuf[cyc, 1]
@@ -389,7 +391,6 @@
         table(merge, 256, 128, 1.0, lambda i, o: ((i & 127) - 32 == o >> 1) & ((i >> 7) == (o & 1)))
         table(t12, 512, 128, 0.125, lambda i, o: (((i & 127) - 32) >> 1 == (o & 31)) & ((i >> 7) == (o >> 5)))
         table(t23, 128, 128, 0.125, lambda i, o: ((i - 48) >> 1) == o - 56)
-        table(u2, 384, 512, 1.0, lambda i, o: (((i & 127) >> 5) == (o >> 7)) & ((o & 127) - 48 == ((i >> 7) - 1) * 32 + (i & 31)))
         table(p32, 128, 128, 1.0, lambda i, o: ((o - 48) >> 1) == i - 56)
         table(p21, 128, 128, 1.0, lambda i, o: ((o - 32) >> 1) == i - 48)
 
@@ -412,8 +413,8 @@
             ref[...] = jnp.zeros(ref.shape, F32)
         clear_r1(bs1, 2, rp1, rs1)
         clear_r1(b2, 1, rp2, rs2)
-        clear_r2(rt1)
-        clear_r2(rt2)
+        clear_r2(rt1, rd1, rx1)
+        clear_r2(rt2, rd2, rx2)
 
     table(split, 128, 256, 1.0, lambda i, o: ((o & 127) - 32 == i >> 1) & ((o >> 7) == (i & 1)))
     for load in loads:
@@ -424,6 +425,9 @@
     link_r = jnp.where(own_ref[0, jnp.minimum(ty + 1, NTY - 1)] == here, 1.0, 0.0)
     link = jnp.where(lane8 == 56, link_l, jnp.where(lane8 == 72, link_r, 1.0))
 
+    bufs1 = (tb1, sd1, st1, rt1, rd1, rx1)
+    bufs2 = (tb2, sd2, st2, rt2, rd2, rx2)
+
     def screen_sums(first, count):
         for i in range(first, first + count):
             even = bs1[1, pl.ds(brow(0, 4 + 2 * i), 32), :]
@@ -431,19 +435,24 @@
             x = even + odd
             ebuf[pl.ds(i * 16, 16), :] = x[:16] + x[16:]
 
+    def put_tile(tb, a, x):
+        tb[0, a] = pltpu.roll(x, 32, 1)
+        tb[1, a] = x
+        tb[2, a] = pltpu.roll(x, 96, 1)
+
     def own_screens():
         screen_sums(4, 16)
         x = ebuf[pl.ds(64, 128, stride=2), :] + ebuf[pl.ds(65, 128, stride=2), :]
         l1e[...] = 0.125 * x
         s2_own = restrict1()
-        for m in (0, 1):
-            m1ud[m, 1] = s2_own
-            m1lr[m, 1] = s2_own
-            m1ud[m, 7] = link
+        put_tile(tb1, 1, s2_own)
+        for m in range(3):
+            tb1[m, 2] = link
         rt1[2, 1, 1] = s2_own
 
-    def vcycle(cyc, src, pk, rp, sl, rs, mud, mlr, rt, x, y):
+    def vcycle(cyc, src, pk, rp, sl, rs, bufs, x, y):
         ns = 2 - cyc
+        tb, sd, st, rt, rd, rx = bufs
 
         def screens1():
             screen_sums(0, 24)
@@ -452,7 +461,7 @@
             l1g[...] = jnp.where(s > 0.0, 0.8 / (s + 3.0), 0.0)
 
         def defect0():
-            per = 24
+            per = 48
 
             def body(i, c):
                 r = 4 + per * i
@@ -486,39 +495,33 @@
         def pack1():
             for m in (0, 1):
                 for k in range(5):
-                    mud[m, ns + k] = l1v[pl.ds(wrow(8 + k + 11 * m), 8), :]
+                    sd[m, k] = l1v[pl.ds(wrow(8 + k + 11 * m), 8), :]
             for j in (0, 1):
                 left, right = z8, z8
                 for g in range(8):
                     v = pltpu.roll(l1v[pl.ds(wrow(8 + 8 * j + g), 8), :], (16 * g - 80) % 128, 1)
                     right = jnp.where(grp8 == g, v, right)
                     left = jnp.where(grp8 == (g + 5) % 8, v, left)
-                mlr[0, ns + j] = left
-                mlr[1, ns + j] = right
+                st[0, j] = left
+                st[1, j] = right
 
         def down1():
             b2_own = restrict1()
-            for m in (0, 1):
-                mud[m, 0] = b2_own
-                mlr[m, 0] = b2_own
+            put_tile(tb, 0, b2_own)
             rt[2, 1, 0] = b2_own
 
         def unpack2():
             for a in range(ns):
-                block = jnp.concatenate(
-                    [
-                        jnp.concatenate([rt[dxi, dyi, a] for dxi in range(5)], axis=0)
-                        for dyi in range(3)
-                    ],
-                    axis=1,
-                )
-                spread = dot_split(block, u2[...])
                 for z in range(4):
-                    part = spread[:, 128 * z : 128 * z + 128]
-                    if a == 0:
-                        l2b[pl.ds(z * 40, 40), :] = part
-                    else:
-                        l2s[pl.ds(z * 40, 40), :] = part
+                    for k in range(5):
+                        x = jnp.where(quarter == (z + 3) % 4, rt[k, 0, a], rt[k, 1, a])
+                        x = jnp.where(quarter == (z + 1) % 4, rt[k, 2, a], x)
+                        x = pltpu.roll(x, (48 - 32 * z) % 128, 1)
+                        row = pl.ds(z * 40 + 8 * k, 8)
+                        if a == 0:
+                            l2b[row, :] = x
+                        else:
+                            l2s[row, :] = jnp.where((lane8 >= 16) & (lane8 < 112), x, 0.0)
 
         def screens3():
             s = l2s[...]
@@ -529,7 +532,7 @@
                 )
             s = restrict2()
             l3g[...] = jnp.where(s > 0.0, 0.8 / (s + 0.75), 0.0)
-            up, down = rt[1, 1, 7], rt[3, 1, 7]
+            up, down = rt[1, 1, 2], rt[3, 1, 2]
             for k, m in enumerate((jnp.where(sub8 < 4, up, link), down)):
                 l3m[0, k] = 0.125 * m
                 l3m[1, k] = pltpu.roll(0.125 * m, 127, 1)
@@ -569,14 +572,14 @@
             for r in range(3, 29):
                 tile, inner = (r - 8) // 16, (r - 8) % 16
                 j, g = inner // 8, inner % 8
-                v = jnp.where(grp8 == g, rt[2 + tile, 0, ns + j], rt[2 + tile, 2, ns + j])
+                v = jnp.where(grp8 == g, rx[1 + tile, 0, j], rx[1 + tile, 1, j])
                 v = pltpu.roll(v, (16 - 16 * g) % 128, 1)
                 if tile == 0:
                     base = l1v[pl.ds(wrow(r), 8), :]
                 elif tile < 0:
-                    base = rt[1, 1, ns + inner - 11]
+                    base = rd[0, inner - 11]
                 else:
-                    base = rt[3, 1, ns + inner]
+                    base = rd[1, inner]
                 l1v[pl.ds(wrow(r), 8), :] = jnp.where(side8, v, base) + l1x[pl.ds(r * 8, 8), :]
 
         def up1():
@@ -593,39 +596,47 @@
                         x[row, :] = x[row, :] + e
                 return c
 
-            lax.fori_loop(0, 20, body, 0, unroll=10)
+            lax.fori_loop(0, 20, body, 0, unroll=20)
 
         wait_r1(pk, rp, sl, rs, cyc)
         stage("unpack0", lambda: unpack0(src, ns, rp, rs, x))
         if cyc == 0:
             stage("screens1", screens1)
-        stage("sweep0pre", lambda: sweep0(x, y, src, 2, 52, 26))
-        sweep0(y, x, src, 2, 52, 26)
+        stage("sweep0pre", lambda: sweep0(x, y, src, 2, 52, 52))
+        sweep0(y, x, src, 2, 52, 52)
         stage("defect0", defect0)
         stage("restrict0", lambda: restrict0(l1b))
         stage("start1", start1)
         stage("sweep1", lambda: sweep1(l1v, l1w))
         sweep1(l1w, l1v)
-        stage("pack1", pack1)
         stage("defect1", defect1)
         stage("down1", down1)
-        each_r2("start", mud, mlr, rt, cyc)
-        each_r2("wait_recv", mud, mlr, rt, cyc)
+        each_r2("start", 0, bufs, cyc)
+        stage("pack1", pack1)
+        each_r2("start", 1, bufs, cyc)
+        sent_r1(pk, rp, sl, rs, cyc)
+        if cyc == 1:
+            for part in (0, 1):
+                each_r2("wait_send", part, bufs1, 0)
+            for i in range(22):
+                ar_copy(0, i).wait_send()
+        each_r2("wait_recv", 0, bufs, cyc)
         stage("unpack2", unpack2)
         if cyc == 0:
             stage("screens3", screens3)
         stage("down2", down2)
         stage("solve3", lambda: solve3(restrict2()))
         stage("up2", up2)
+        each_r2("wait_recv", 1, bufs, cyc)
         stage("correct1", correct1)
         sweep1(l1v, l1w)
         sweep1(l1w, l1v)
         sweep1(l1v, l1w)
         stage("up1", up1)
         stage("correct0", correct0)
-        stage("sweep0post", lambda: sweep0(x, y, src, 8, 40, 20))
-        sweep0(y, x, src, 10, 36, 18)
-        sweep0(x, y, src, 10, 36, 18)
+        stage("sweep0post", lambda: sweep0(x, y, src, 8, 40, 40))
+        sweep0(y, x, src, 10, 36, 36)
+        sweep0(x, y, src, 10, 36, 36)
 
     def restrict2():
         parts = [
@@ -663,13 +674,26 @@
     stage("prepare", prepare)
     stage("own_screens", own_screens)
 
-    vcycle(0, bs1, pk1, rp1, sl1, rs1, m1ud, m1lr, rt1, va, vb)
+    def merged(i, planes, start):
+        def body(j, c):
+            rows = []
+            for k in range(16):
+                r = TOP + 16 * j + k
+                rows.append(jnp.concatenate([planes[pl.ds(start(t, r), 16), :] for t in (0, 1)], axis=1))
+            x = dot_exact(jnp.concatenate(rows, axis=0), merge[...])
+            for k in range(16):
+                natural[i, pl.ds(16 * j + k, 16, stride=32), :] = x[16 * k : 16 * k + 16]
+            return c
+
+        lax.fori_loop(0, 2, body, 0)
+
+    vcycle(0, bs1, pk1, rp1, sl1, rs1, bufs1, va, vb)
 
     def halves(a):
         return a[0:8] + a[8:16]
 
     def apply_first(i, acc):
-        r = TOP + 16 * i
+        r = TOP + 32 * i
         acc = list(acc)
 
         def put(k, t, c, n):
@@ -679,16 +703,18 @@
             acc[0] = acc[0] + halves(bs1[0, row, :] * c)
             acc[1] = acc[1] + halves(c * q)
 
-        stencil0(vb, r, 16, put)
+        stencil0(vb, r, 32, put)
         return tuple(acc)
 
-    sums = lax.fori_loop(0, 2, apply_first, (z8, z8))
+    sums = lax.fori_loop(0, 1, apply_first, (z8, z8))
     stage("pack0x1", lambda: pack0(b2, 1, pk2, sl2))
     start_r1(pk2, rp2, sl2, rs2, 1)
     ar_begin(0, sums)
+    stage("merged", lambda: merged(0, vb, vrow))
+    merged(1, b2.at[0], brow)
     ar_middle(0)
 
-    vcycle(1, b2, pk2, rp2, sl2, rs2, m2ud, m2lr, rt2, va, vc)
+    vcycle(1, b2, pk2, rp2, sl2, rs2, bufs2, va, vc)
     rho0, curv0 = ar_end(0, 2)
     step0 = rho0 / curv0
     step0_16 = jnp.concatenate([step0, step0], axis=0)
@@ -700,10 +726,10 @@
                 vc[row, :] = vb[row, :] - step0_16 * vc[row, :]
         return c
 
-    lax.fori_loop(0, 18, next_z, 0, unroll=9)
+    lax.fori_loop(0, 18, next_z, 0, unroll=18)
 
     def apply_second(i, acc):
-        r = TOP + 16 * i
+        r = TOP + 32 * i
         acc = list(acc)
 
         def put(k, t, c, n):
@@ -716,11 +742,13 @@
             acc[1] = acc[1] + halves(c * q)
             acc[2] = acc[2] + halves(c * q0 + z0 * q)
 
-        stencil0(vc, r, 16, put)
+        stencil0(vc, r, 32, put)
         return tuple(acc)
 
-    sums = lax.fori_loop(0, 2, apply_second, (z8, z8, z8))
+    sums = lax.fori_loop(0, 1, apply_second, (z8, z8, z8))
     ar_begin(1, sums)
+    merged(2, vc, vrow)
+    merged(3, q1, brow)
     ar_middle(1)
     rho1, zz, cross = ar_end(1, 3)
     beta = rho1 / rho0
@@ -728,43 +756,15 @@
     step1 = rho1 / curv1
     mixed = step0 + step1 * beta
 
-    def finish():
-        mixed_16 = jnp.concatenate([mixed, mixed], axis=0)
-        step1_16 = jnp.concatenate([step1, step1], axis=0)
-
-        def body(i, c):
-            sol, app = [], []
-            for k in range(8):
-                r = TOP + 8 * i + k
-                z, q = [], []
-                for t in (0, 1):
-                    v, b = pl.ds(vrow(t, r), 16), pl.ds(brow(t, r), 16)
-                    z.append(mixed_16 * vb[v, :] + step1_16 * vc[v, :])
-                    q.append(mixed_16 * b2[0, b, :] + step1_16 * q1[b, :])
-                sol.append(jnp.concatenate(z, axis=1))
-                app.append(jnp.concatenate(q, axis=1))
-            for a, rows in ((0, sol), (1, app)):
-                natural[a] = dot_exact(jnp.concatenate(rows, axis=0), merge[...])
-            at_rows = pl.ds(pl.multiple_of(8 * i, 8), 8)
-            for z in range(16):
-                sol_ref[z, at_rows, :] = natural[0, pl.ds(z, 8, stride=16), :]
-                res_ref[z, at_rows, :] = (
-                    rhs_ref[pl.ds(pl.multiple_of(z * 32 + 8 * i, 8), 8), :]
-                    - natural[1, pl.ds(z, 8, stride=16), :]
-                )
-            return c
-
-        lax.fori_loop(0, 4, body, 0)
-
-    stage("finish", finish)
-
-    sent_r1(pk1, rp1, sl1, rs1, 0)
-    sent_r1(pk2, rp2, sl2, rs2, 1)
-    each_r2("wait_send", m1ud, m1lr, rt1, 0)
-    each_r2("wait_send", m2ud, m2lr, rt2, 1)
-    for cyc in (0, 1):
-        for i in range(22):
-            ar_copy(cyc, i).wait_send()
+    for k in range(0, 512, 8):
+        row = pl.ds(k, 8)
+        sol_ref[row, :] = mixed * natural[0, row, :] + step1 * natural[2, row, :]
+        res_ref[row, :] = rhs_ref[row, :] - mixed * natural[1, row, :] - step1 * natural[3, row, :]
+
+    for part in (0, 1):
+        each_r2("wait_send", part, bufs2, 1)
+    for i in range(7, 22):
+        ar_copy(1, i).wait_send()
 
 
 def on_device(right_side, screening, owners):
@@ -778,33 +778,34 @@
         vm(padded, 128), vm(padded, 128), vm(padded, 128), vm(2 * PLANE, 128),
         vm(2, 2, 64, 128), vm(2, 1, 64, 128), vm(3, 2, 2, 64, 128), vm(3, 2, 1, 64, 128),
         vm(2, 2, HALO * 16, 128), vm(2, 1, HALO * 16, 128), vm(2, 2, HALO * 16, 128), vm(2, 1, HALO * 16, 128),
-        vm(24 * 16, 128), vm(20 * 16, 128), vm(2, 128, 128),
+        vm(24 * 16, 128), vm(20 * 16, 128), vm(4, 512, 128),
         vm(R1 * 8, 128), vm(R1 * 8, 128), vm(R1 * 8, 128), vm(R1 * 8, 128),
         vm(R1 * 16 + 16, 128), vm(R1 * 16 + 16, 128), vm(128, 128),
-        vm(2, 8, 8, 128), vm(2, 4, 8, 128), vm(2, 8, 8, 128), vm(2, 4, 8, 128),
-        vm(5, 3, 8, 8, 128), vm(5, 3, 8, 8, 128),
+        vm(3, 3, 8, 128), vm(3, 1, 8, 128), vm(2, 5, 8, 128), vm(2, 5, 8, 128), vm(2, 2, 8, 128), vm(2, 2, 8, 128),
+        vm(5, 3, 3, 8, 128), vm(5, 3, 1, 8, 128), vm(2, 5, 8, 128), vm(2, 5, 8, 128),
+        vm(3, 2, 2, 8, 128), vm(3, 2, 2, 8, 128),
         vm(160, 128), vm(160, 128), vm(160, 128), vm(4 * 56, 128), vm(4 * 56, 128),
         vm(80, 128), vm(64, 128), vm(32, 128), vm(2, 2, 8, 128),
-        bm(128, 256), bm(256, 128), bm(512, 128), bm(384, 512), bm(128, 128), bm(128, 128), bm(128, 128),
+        bm(128, 256), bm(256, 128), bm(512, 128), bm(128, 128), bm(128, 128), bm(128, 128),
         vm(2, 2, 1, 128), vm(2, 7, 1, 128), vm(2, 15, 1, 128),
         pltpu.SemaphoreType.DMA((2, 8)), pltpu.SemaphoreType.DMA((2, 8)),
-        pltpu.SemaphoreType.DMA((2, 14)), pltpu.SemaphoreType.DMA((2, 14)),
+        pltpu.SemaphoreType.DMA((2, 22)), pltpu.SemaphoreType.DMA((2, 22)),
         pltpu.SemaphoreType.DMA((2, 22)), pltpu.SemaphoreType.DMA((2, 22)),
     ]
-    block = jax.ShapeDtypeStruct(right_side.shape, F32)
+    field = pltpu.VMEM((512, 128), F32)
     vmem = pl.BlockSpec(memory_space=pltpu.VMEM)
-    return tuple(
-        pl.pallas_call(
-            kernel,
-            out_shape=(block, block),
-            in_specs=[pl.BlockSpec(memory_space=pl.ANY)] * 3,
-            out_specs=(vmem, vmem),
-            scratch_shapes=scratch,
-            compiler_params=pltpu.CompilerParams(
-                collective_id=0, has_side_effects=True, vmem_limit_bytes=60 * 2**20
-            ),
-        )(right_side.reshape(512, 128), screening.reshape(512, 128), owners)
-    )
+    hbm = lambda x: pltpu.with_memory_space_constraint(x, pltpu.HBM)
+    out = pl.pallas_call(
+        kernel,
+        out_shape=(field, field),
+        in_specs=[pl.BlockSpec(memory_space=pltpu.HBM)] * 3,
+        out_specs=(vmem, vmem),
+        scratch_shapes=scratch,
+        compiler_params=pltpu.CompilerParams(
+            collective_id=0, has_side_effects=True, vmem_limit_bytes=40 * 2**20
+        ),
+    )(hbm(right_side.reshape(512, 128)), hbm(screening.reshape(512, 128)), hbm(owners))
+    return tuple(x.reshape(right_side.shape) for x in out)
 
 
 def solution(mesh):

time: 55.1 us -> 49.5 us (0.90)
  Pallas kernels: 51.9 us -> 47.3 us
  local copies, waits for them, and re-layouts: 2.42 us -> 1.41 us
    pallas_call x1, Pallas kernels: 51.9 us -> 47.3 us  [on_device(): pl.pallas_call(kernel, out_shape=(field, field), in_specs=[pl.BlockSpec(m...]
    unnamed x4 -> x2, local copies, waits for them, and re-layouts: 2.42 us -> 1.41 us
where the time goes in v3:
time: 49.5 us; the launch traced here: 49.3 us
  Pallas kernels  47.3 us (96%)
  local copies, waits for them, and re-layouts  1.41 us (3%)
  between operations  0.64 us (1%)
    pallas_call x1, Pallas kernels, on_device(): pl.pallas_call(kernel, out_shape=(field, field), in_specs=[pl.BlockSpec(m...  47.3 us
    unnamed x2, local copies, waits for them, and re-layouts  1.41 us

profile of v3, /device:TPU:0, one launch (start us, length us, event | category | flops | bytes accessed | tf_op | source)
XLA Modules:
  0.0 49.3 jit_solution(5947968015758151493)
XLA Ops:
  0.6 47.3 %shard_map.50 = (f32[512,128]{1,0:T(8,128)S(1)}, f32[512,128]{1,0:T(8,128)S(1)}) custom-call(f32[512,128]{1,0:T(8,128)} %bitcast.6, f32[512,128]{1,0:T(8,128)} %bitcast.7, s32[1,16]{1,0:T(1,128)} %own_hbm.1), custom_call_target="tpu_custom_call" | custom-call | tf_op jit(solution)/shard_map/pallas_call | solution.py:798
  47.9 0.7 %copy.7 = f32[16,32,128]{2,1,0:T(8,128)} copy(f32[16,32,128]{2,1,0:T(8,128)S(1)} %bitcast.5) | data formatting | bytes 524288
  48.6 0.7 %copy.8 = f32[16,32,128]{2,1,0:T(8,128)} copy(f32[16,32,128]{2,1,0:T(8,128)S(1)} %bitcast.4) | data formatting | bytes 524288

commit v4 on v3

--- a/solution.py
+++ b/solution.py
@@ -43,9 +43,9 @@
 
 
 def kernel(
-    rhs_hbm, scr_hbm, own_hbm, sol_ref, res_ref,
+    rhs_hbm, scr_hbm, own_hbm, out_ref,
     rhs_ref, scr_ref, own_ref, s_in,
-    bs1, b2, gain, va, vb, vc, q1, pk1, pk2, rp1, rp2, sl1, sl2, rs1, rs2, ebuf, xbuf, natural,
+    bs1, b2, gain, va, vb, vc, q1, pk1, pk2, rp1, rp2, sl1, sl2, rs1, rs2, natural,
     l1s, l1g, l1b, l1x, l1v, l1w, l1e,
     tb1, tb2, sd1, sd2, st1, st2, rt1, rt2, rd1, rd2, rx1, rx2,
     l2b, l2s, l2g, l2v, l2w, l2e, l2x, l3g, l3m,
@@ -75,7 +75,7 @@
     def ring(dx, dy):
         return {"tx": lax.rem(tx + dx, NTX), "ty": lax.rem(ty + dy, NTY)}
 
-    ring_dirs = [(k, 0) for k in range(1, NTX)] + [(0, k) for k in range(1, NTY)]
+    ring_dirs = [(0, k) for k in range(1, NTY)] + [(k, 0) for k in range(1, NTX)]
     extra = [d for d in DIRS14 if d[0] != 0 and d[1] != 0]
     expected = jnp.int32(len(ring_dirs))
     for d in ring_dirs:
@@ -113,7 +113,7 @@
     def take_inputs():
         for a, ref in enumerate((rhs_ref, scr_ref)):
             for i in range(2):
-                x = [ref[pl.ds(16 * i + k, 16, stride=32), :] for k in range(16)]
+                x = [ref[pl.ds(16 * i + k + z, 8, stride=64), :] for k in range(16) for z in (32, 0)]
                 x = dot_exact(jnp.concatenate(x, axis=0), split[...])
                 for t in (0, 1):
                     at_row = (t * ROWS + TOP + 16 * i) * 16
@@ -313,9 +313,14 @@
             beside = (odd + pltpu.roll(odd, 1, 1), even + pltpu.roll(even, 127, 1))
             for t in (0, 1):
                 at_row = vrow(t, r + k)
+                c = rows[t][k + 1]
+                depth = [
+                    c[8:] + src[pl.ds(at_row + 9, 8), :],
+                    c[:8] + src[pl.ds(at_row - 1, 8), :],
+                ]
                 n = rows[t][k] + rows[t][k + 2]
-                n = n + (src[pl.ds(at_row - 1, 16), :] + src[pl.ds(at_row + 1, 16), :])
-                put(k, t, rows[t][k + 1], n + beside[t])
+                n = n + jnp.concatenate(depth, axis=0)
+                put(k, t, c, n + beside[t])
 
     def sweep0(src, dst, bref, r0, count, per):
         def body(i, carry):
@@ -330,9 +335,8 @@
 
         lax.fori_loop(0, count // per, body, 0)
 
-    def restrict0(out):
-        x = ebuf[pl.ds(0, 192, stride=2), :] + ebuf[pl.ds(1, 192, stride=2), :]
-        out[pl.ds(32, 192), :] = 0.125 * x
+    def folded(x):
+        return 0.125 * (x[:8] + x[8:])
 
     def wrow(r):
         return pl.multiple_of(8 + r * 16, 8)
@@ -428,12 +432,12 @@
     bufs1 = (tb1, sd1, st1, rt1, rd1, rx1)
     bufs2 = (tb2, sd2, st2, rt2, rd2, rx2)
 
-    def screen_sums(first, count):
+    def screen_sums(first, count, out, base):
         for i in range(first, first + count):
             even = bs1[1, pl.ds(brow(0, 4 + 2 * i), 32), :]
             odd = bs1[1, pl.ds(brow(1, 4 + 2 * i), 32), :]
             x = even + odd
-            ebuf[pl.ds(i * 16, 16), :] = x[:16] + x[16:]
+            out[pl.ds((base + i) * 8, 8), :] = folded(x[:16] + x[16:])
 
     def put_tile(tb, a, x):
         tb[0, a] = pltpu.roll(x, 32, 1)
@@ -441,9 +445,7 @@
         tb[2, a] = pltpu.roll(x, 96, 1)
 
     def own_screens():
-        screen_sums(4, 16)
-        x = ebuf[pl.ds(64, 128, stride=2), :] + ebuf[pl.ds(65, 128, stride=2), :]
-        l1e[...] = 0.125 * x
+        screen_sums(4, 16, l1e, -4)
         s2_own = restrict1()
         put_tile(tb1, 1, s2_own)
         for m in range(3):
@@ -455,8 +457,7 @@
         tb, sd, st, rt, rd, rx = bufs
 
         def screens1():
-            screen_sums(0, 24)
-            restrict0(l1s)
+            screen_sums(0, 24, l1s, 4)
             s = l1s[...]
             l1g[...] = jnp.where(s > 0.0, 0.8 / (s + 3.0), 0.0)
 
@@ -471,8 +472,8 @@
                     row = pl.ds(brow(t, r + k), 16)
                     held.append(src[0, row, :] - (bs1[1, row, :] + 6.0) * centre + n)
                     if len(held) == 4:
-                        at_row = pl.multiple_of((i * (per // 2) + k // 2) * 16, 16)
-                        ebuf[pl.ds(at_row, 16), :] = (held[0] + held[1]) + (held[2] + held[3])
+                        at_row = pl.multiple_of((4 + i * (per // 2) + k // 2) * 8, 8)
+                        l1b[pl.ds(at_row, 8), :] = folded((held[0] + held[1]) + (held[2] + held[3]))
                         held.clear()
 
                 stencil0(x, r, per, put)
@@ -582,14 +583,10 @@
                     base = rd[1, inner]
                 l1v[pl.ds(wrow(r), 8), :] = jnp.where(side8, v, base) + l1x[pl.ds(r * 8, 8), :]
 
-        def up1():
-            e1 = jnp.concatenate([l1w[pl.ds(wrow(6 + k), 8), :] for k in range(20)], axis=0)
-            for b in (0, 1):
-                xbuf[pl.ds(b, 160, stride=2), :] = e1
-
         def correct0():
             def body(i, c):
-                e = xbuf[pl.ds(pl.multiple_of(i * 16, 16), 16), :]
+                e = l1w[pl.ds(wrow(6 + i), 8), :]
+                e = jnp.concatenate([e, e], axis=0)
                 for t in (0, 1):
                     for k in (0, 1):
                         row = pl.ds(vrow(t, 8 + 2 * i + k), 16)
@@ -603,9 +600,8 @@
         if cyc == 0:
             stage("screens1", screens1)
         stage("sweep0pre", lambda: sweep0(x, y, src, 2, 52, 52))
-        sweep0(y, x, src, 2, 52, 52)
+        sweep0(y, x, src, 3, 50, 50)
         stage("defect0", defect0)
-        stage("restrict0", lambda: restrict0(l1b))
         stage("start1", start1)
         stage("sweep1", lambda: sweep1(l1v, l1w))
         sweep1(l1w, l1v)
@@ -616,6 +612,8 @@
         each_r2("start", 1, bufs, cyc)
         sent_r1(pk, rp, sl, rs, cyc)
         if cyc == 1:
+            merged(0, vb, vrow)
+            merged(1, b2.at[0], brow)
             for part in (0, 1):
                 each_r2("wait_send", part, bufs1, 0)
             for i in range(22):
@@ -632,11 +630,10 @@
         sweep1(l1v, l1w)
         sweep1(l1w, l1v)
         sweep1(l1v, l1w)
-        stage("up1", up1)
         stage("correct0", correct0)
-        stage("sweep0post", lambda: sweep0(x, y, src, 8, 40, 40))
+        stage("sweep0post", lambda: sweep0(x, y, src, 9, 38, 38))
         sweep0(y, x, src, 10, 36, 36)
-        sweep0(x, y, src, 10, 36, 36)
+        sweep0(x, y, src, 11, 34, 34)
 
     def restrict2():
         parts = [
@@ -682,7 +679,9 @@
                 rows.append(jnp.concatenate([planes[pl.ds(start(t, r), 16), :] for t in (0, 1)], axis=1))
             x = dot_exact(jnp.concatenate(rows, axis=0), merge[...])
             for k in range(16):
-                natural[i, pl.ds(16 * j + k, 16, stride=32), :] = x[16 * k : 16 * k + 16]
+                r = 16 * j + k
+                natural[i, pl.ds(r + 32, 8, stride=64), :] = x[16 * k : 16 * k + 8]
+                natural[i, pl.ds(r, 8, stride=64), :] = x[16 * k + 8 : 16 * k + 16]
             return c
 
         lax.fori_loop(0, 2, body, 0)
@@ -710,8 +709,6 @@
     stage("pack0x1", lambda: pack0(b2, 1, pk2, sl2))
     start_r1(pk2, rp2, sl2, rs2, 1)
     ar_begin(0, sums)
-    stage("merged", lambda: merged(0, vb, vrow))
-    merged(1, b2.at[0], brow)
     ar_middle(0)
 
     vcycle(1, b2, pk2, rp2, sl2, rs2, bufs2, va, vc)
@@ -758,8 +755,8 @@
 
     for k in range(0, 512, 8):
         row = pl.ds(k, 8)
-        sol_ref[row, :] = mixed * natural[0, row, :] + step1 * natural[2, row, :]
-        res_ref[row, :] = rhs_ref[row, :] - mixed * natural[1, row, :] - step1 * natural[3, row, :]
+        out_ref[0, row, :] = mixed * natural[0, row, :] + step1 * natural[2, row, :]
+        out_ref[1, row, :] = rhs_ref[row, :] - mixed * natural[1, row, :] - step1 * natural[3, row, :]
 
     for part in (0, 1):
         each_r2("wait_send", part, bufs2, 1)
@@ -778,7 +775,7 @@
         vm(padded, 128), vm(padded, 128), vm(padded, 128), vm(2 * PLANE, 128),
         vm(2, 2, 64, 128), vm(2, 1, 64, 128), vm(3, 2, 2, 64, 128), vm(3, 2, 1, 64, 128),
         vm(2, 2, HALO * 16, 128), vm(2, 1, HALO * 16, 128), vm(2, 2, HALO * 16, 128), vm(2, 1, HALO * 16, 128),
-        vm(24 * 16, 128), vm(20 * 16, 128), vm(4, 512, 128),
+        vm(4, 512, 128),
         vm(R1 * 8, 128), vm(R1 * 8, 128), vm(R1 * 8, 128), vm(R1 * 8, 128),
         vm(R1 * 16 + 16, 128), vm(R1 * 16 + 16, 128), vm(128, 128),
         vm(3, 3, 8, 128), vm(3, 1, 8, 128), vm(2, 5, 8, 128), vm(2, 5, 8, 128), vm(2, 2, 8, 128), vm(2, 2, 8, 128),
@@ -792,20 +789,19 @@
         pltpu.SemaphoreType.DMA((2, 22)), pltpu.SemaphoreType.DMA((2, 22)),
         pltpu.SemaphoreType.DMA((2, 22)), pltpu.SemaphoreType.DMA((2, 22)),
     ]
-    field = pltpu.VMEM((512, 128), F32)
     vmem = pl.BlockSpec(memory_space=pltpu.VMEM)
     hbm = lambda x: pltpu.with_memory_space_constraint(x, pltpu.HBM)
     out = pl.pallas_call(
         kernel,
-        out_shape=(field, field),
+        out_shape=pltpu.VMEM((2, 512, 128), F32),
         in_specs=[pl.BlockSpec(memory_space=pltpu.HBM)] * 3,
-        out_specs=(vmem, vmem),
+        out_specs=vmem,
         scratch_shapes=scratch,
         compiler_params=pltpu.CompilerParams(
             collective_id=0, has_side_effects=True, vmem_limit_bytes=40 * 2**20
         ),
     )(hbm(right_side.reshape(512, 128)), hbm(screening.reshape(512, 128)), hbm(owners))
-    return tuple(x.reshape(right_side.shape) for x in out)
+    return out[0].reshape(right_side.shape), out[1].reshape(right_side.shape)
 
 
 def solution(mesh):

time: 49.5 us -> 48.4 us (0.978)
  local copies, waits for them, and re-layouts: 1.41 us -> 0.82 us
  Pallas kernels: 47.3 us -> 46.8 us
    unnamed x2 -> x0, local copies, waits for them, and re-layouts: 1.41 us -> none
    slice x0 -> x1, local copies, waits for them, and re-layouts: none -> 0.82 us  [on_device(): return (out[0].reshape(right_side.shape), out[1].reshape(right_side.shape))]
    pallas_call x1, Pallas kernels: 47.3 us -> 46.8 us  [on_device(): pl.pallas_call(kernel, out_shape=pltpu.VMEM((2, 512, 128), F32), in_specs...]
where the time goes in v4:
time: 48.4 us; the launch traced here: 48.3 us
  Pallas kernels  46.8 us (97%)
  local copies, waits for them, and re-layouts  0.82 us (2%)
  between operations  0.64 us (1%)
    pallas_call x1, Pallas kernels, on_device(): pl.pallas_call(kernel, out_shape=pltpu.VMEM((2, 512, 128), F32), in_specs...  46.8 us

profile of v4, /device:TPU:0, one launch (start us, length us, event | category | flops | bytes accessed | tf_op | source)
XLA Modules:
  0.0 48.3 jit_solution(4341449315842440691)
XLA Ops:
  0.6 46.8 %shard_map.50 = f32[2,512,128]{2,1,0:T(8,128)S(1)} custom-call(f32[512,128]{1,0:T(8,128)} %bitcast.4, f32[512,128]{1,0:T(8,128)} %bitcast.5, s32[1,16]{1,0:T(1,128)} %own_hbm.1), custom_call_target="tpu_custom_call" | custom-call | tf_op jit(solution)/shard_map/pallas_call | solution.py:794
  47.4 0.8 %fusion = (f32[1,512,128]{2,1,0:T(8,128)}, f32[1,512,128]{2,1,0:T(8,128)}) fusion(f32[2,512,128]{2,1,0:T(8,128)S(1)} %shard_map.50), kind=kLoop, calls=%fused_computation | loop fusion | bytes 1048576 | tf_op jit(solution)/shard_map/slice | solution.py:804

commit v5 on v4

--- a/solution.py
+++ b/solution.py
@@ -93,10 +93,15 @@
     sub8 = iota((8, 128), 0)
     grp8 = lane8 >> 4
     quarter = lane8 >> 5
-    half16 = lane16 >> 3
     own16 = (lane16 >= 32) & (lane16 < 96)
     own8 = (lane8 >= 32) & (lane8 < 96)
-    side16 = ((lane16 >= 24) & (lane16 < 32)) | ((lane16 >= 96) & (lane16 < 104))
+
+    def span16(first, count):
+        return ((lane16 - first) & 127) < count
+
+    side_even = span16(27, 5) | span16(96, 6)
+    side_odd = span16(26, 6) | span16(96, 5)
+    packed_rows = ((0, 11), (11, 10), (21, 11))
     side8 = ((lane8 >= 16) & (lane8 < 32)) | ((lane8 >= 96) & (lane8 < 112))
     z16 = jnp.zeros((16, 128), F32)
     z8 = jnp.zeros((8, 128), F32)
@@ -119,23 +124,21 @@
                     at_row = (t * ROWS + TOP + 16 * i) * 16
                     bs1[a, pl.ds(at_row, 256), :] = x[:, 128 * t : 128 * t + 128]
 
-    def pack0(src, count, pk, sl):
-        for j in range(4):
-            span = pl.ds(pl.multiple_of(j * 16, 16), 16)
+    def pack0(src, count, pk):
+        for j, (r0, rows) in enumerate(packed_rows):
+            span = pl.ds(j * 16, 16)
             for a in range(count):
                 left, right = z16, z16
-                for g in range(8):
-                    even = src[a, pl.ds(brow(0, TOP + j * 8 + g), 16), :]
-                    odd = src[a, pl.ds(brow(1, TOP + j * 8 + g), 16), :]
-                    even = pltpu.roll(even, (16 * g - 88) % 128, 1)
-                    odd = pltpu.roll(odd, (16 * g - 80) % 128, 1)
-                    right = jnp.where(half16 == 2 * g, even, jnp.where(half16 == 2 * g + 1, odd, right))
-                    left = jnp.where(
-                        half16 == (2 * g - 7) % 16, even,
-                        jnp.where(half16 == (2 * g - 6) % 16, odd, left),
-                    )
+                for g in range(rows):
+                    even = src[a, pl.ds(brow(0, TOP + r0 + g), 16), :]
+                    odd = src[a, pl.ds(brow(1, TOP + r0 + g), 16), :]
+                    even = pltpu.roll(even, (11 * g - 91) % 128, 1)
+                    odd = pltpu.roll(odd, (11 * g - 85) % 128, 1)
+                    right = jnp.where(span16(11 * g, 5), even, jnp.where(span16(11 * g + 5, 6), odd, right))
+                    left = jnp.where(span16(11 * g + 69, 6), even, jnp.where(span16(11 * g + 75, 5), odd, left))
                 pk[0, a, span, :] = left
                 pk[1, a, span, :] = right
+    def pack_slabs(src, count, sl):
         for a in range(count):
             for m, first in ((0, TOP), (1, TOP + 32 - HALO)):
                 for k in range(HALO):
@@ -145,20 +148,19 @@
 
     def unpack0(dst, count, rp, rs, x):
         def row(dxi, j, g):
-            r = TOP + (dxi - 1) * 32 + j * 8 + g
-            span = pl.ds(pl.multiple_of(j * 16, 16), 16)
+            r = TOP + (dxi - 1) * 32 + packed_rows[j][0] + g
+            span = pl.ds(j * 16, 16)
             out = []
             for a in range(count):
                 fl, fr = rp[dxi, 0, a, span, :], rp[dxi, 1, a, span, :]
                 if dxi == 1:
                     even, odd = dst[a, pl.ds(brow(0, r), 16), :], dst[a, pl.ds(brow(1, r), 16), :]
                 else:
-                    k = j * 8 + g - (32 - HALO if dxi == 0 else 0)
-                    both = rs[dxi // 2, a, pl.ds(16 * k, 16), :]
+                    both = rs[dxi // 2, a, pl.ds(16 * g, 16), :]
                     even, odd = jnp.where(own16, both, 0.0), jnp.where(own16, pltpu.roll(both, 64, 1), 0.0)
-                ve = pltpu.roll(jnp.where(half16 == 2 * g, fl, fr), (24 - 16 * g) % 128, 1)
-                vo = pltpu.roll(jnp.where(half16 == 2 * g + 1, fl, fr), (16 - 16 * g) % 128, 1)
-                even, odd = jnp.where(side16, ve, even), jnp.where(side16, vo, odd)
+                ve = pltpu.roll(jnp.where(span16(11 * g, 5), fl, fr), (27 - 11 * g) % 128, 1)
+                vo = pltpu.roll(jnp.where(span16(11 * g + 5, 6), fl, fr), (21 - 11 * g) % 128, 1)
+                even, odd = jnp.where(side_even, ve, even), jnp.where(side_odd, vo, odd)
                 dst[a, pl.ds(brow(0, r), 16), :] = even
                 dst[a, pl.ds(brow(1, r), 16), :] = odd
                 out.append((even, odd))
@@ -172,15 +174,10 @@
                     gv = gain[at_row, :]
                 x[pl.ds(vrow(t, r), 16), :] = gv * out[0][t]
 
-        for j in range(4):
-            for g in range(8):
-                row(1, j, g)
-        for j, groups in ((2, range(5, 8)), (3, range(8))):
-            for g in groups:
-                row(0, j, g)
-        for j, groups in ((0, range(8)), (1, range(3))):
-            for g in groups:
-                row(2, j, g)
+        for dxi, js in ((1, (0, 1, 2)), (0, (2,)), (2, (0,))):
+            for j in js:
+                for g in range(packed_rows[j][1]):
+                    row(dxi, j, g)
 
     def r1_copy(i, d, pk, rp, sl, rs, cyc):
         dx, dy = d
@@ -191,16 +188,19 @@
             if dx == 0:
                 s, t = pk.at[side], rp.at[1, 1 - side]
             elif dx == -1:
-                s, t = pk.at[side, :, pl.ds(0, 32)], rp.at[2, 1 - side, :, pl.ds(0, 32)]
+                s, t = pk.at[side, :, pl.ds(0, 16)], rp.at[2, 1 - side, :, pl.ds(0, 16)]
             else:
-                s, t = pk.at[side, :, pl.ds(32, 32)], rp.at[0, 1 - side, :, pl.ds(32, 32)]
+                s, t = pk.at[side, :, pl.ds(32, 16)], rp.at[0, 1 - side, :, pl.ds(32, 16)]
         return pltpu.make_async_remote_copy(
             src_ref=s, dst_ref=t, send_sem=s_r1.at[cyc, i], recv_sem=r_r1.at[cyc, i],
             device_id=at(*d), device_id_type=MESH,
         )
 
-    def start_r1(pk, rp, sl, rs, cyc):
+    def start_r1(pk, rp, sl, rs, cyc, slabs):
         for i, d in enumerate(DIRS8):
+            if (d[1] == 0) != slabs:
+                continue
+
             @pl.when(inside(*d))
             def _():
                 r1_copy(i, d, pk, rp, sl, rs, cyc).start()
@@ -230,13 +230,14 @@
             for sidei, dy in ((0, -1), (1, 1)):
                 @pl.when(jnp.logical_not(inside(dxi - 1, dy)))
                 def _():
-                    rp[dxi, sidei] = jnp.zeros((count, 64, 128), F32)
+                    rp[dxi, sidei] = jnp.zeros((count, 48, 128), F32)
 
     def r2_copy(i, d, bufs, cyc):
         tb, sd, st, rt, rd, rx = bufs
         dx, dy = d
         if i < 14:
-            s, t = tb.at[1 + dy], rt.at[2 - dx, 1 - dy]
+            n = 3 if cyc == 0 and abs(dx) == 1 and dy == 0 else 2 - cyc
+            s, t = tb.at[1 + dy, pl.ds(0, n)], rt.at[2 - dx, 1 - dy, pl.ds(0, n)]
         elif dy == 0:
             s, t = sd.at[0 if dx < 0 else 1], rd.at[1 if dx < 0 else 0]
         else:
@@ -280,7 +281,7 @@
             acc = jnp.sum(jnp.where(own8, acc, 0.0), axis=0, keepdims=True)
             out = jnp.where(lane8[:1] == k, jnp.sum(acc, axis=1, keepdims=True), out)
         arbuf[cyc, 0] = out
-        for i in range(7):
+        for i in (3, 2, 4, 1, 5, 6, 0):
             ar_copy(cyc, i).start()
 
     def ar_middle(cyc):
@@ -290,8 +291,8 @@
         for i in range(7):
             total = total + arr1[cyc, i]
         arbuf[cyc, 1] = total
-        for i in range(7, 22):
-            ar_copy(cyc, i).start()
+        for k in (10, 6, 9, 11, 5, 7, 14, 2, 8, 13, 3, 12, 4, 15, 1):
+            ar_copy(cyc, 6 + k).start()
         if cyc == 1:
             for i in range(7):
                 ar_copy(cyc, i).wait_send()
@@ -448,8 +449,7 @@
         screen_sums(4, 16, l1e, -4)
         s2_own = restrict1()
         put_tile(tb1, 1, s2_own)
-        for m in range(3):
-            tb1[m, 2] = link
+        tb1[1, 2] = link
         rt1[2, 1, 1] = s2_own
 
     def vcycle(cyc, src, pk, rp, sl, rs, bufs, x, y):
@@ -665,9 +665,11 @@
             for a in (0, 1):
                 l2x[pl.ds(z * 32 + a, 16, stride=2), :] = e3[16 * z : 16 * z + 16]
 
-    stage("pack0x2", lambda: pack0(bs1, 2, pk1, sl1))
+    pack0(bs1, 2, pk1)
+    pack_slabs(bs1, 2, sl1)
     pl.semaphore_wait(barrier, expected)
-    start_r1(pk1, rp1, sl1, rs1, 0)
+    start_r1(pk1, rp1, sl1, rs1, 0, False)
+    start_r1(pk1, rp1, sl1, rs1, 0, True)
     stage("prepare", prepare)
     stage("own_screens", own_screens)
 
@@ -706,8 +708,10 @@
         return tuple(acc)
 
     sums = lax.fori_loop(0, 1, apply_first, (z8, z8))
-    stage("pack0x1", lambda: pack0(b2, 1, pk2, sl2))
-    start_r1(pk2, rp2, sl2, rs2, 1)
+    pack0(b2, 1, pk2)
+    start_r1(pk2, rp2, sl2, rs2, 1, False)
+    pack_slabs(b2, 1, sl2)
+    start_r1(pk2, rp2, sl2, rs2, 1, True)
     ar_begin(0, sums)
     ar_middle(0)
 
@@ -773,7 +777,7 @@
         pltpu.SemaphoreType.DMA((3,)),
         vm(2, 2 * PLANE, 128), vm(1, 2 * PLANE, 128), vm(2 * PLANE, 128),
         vm(padded, 128), vm(padded, 128), vm(padded, 128), vm(2 * PLANE, 128),
-        vm(2, 2, 64, 128), vm(2, 1, 64, 128), vm(3, 2, 2, 64, 128), vm(3, 2, 1, 64, 128),
+        vm(2, 2, 48, 128), vm(2, 1, 48, 128), vm(3, 2, 2, 48, 128), vm(3, 2, 1, 48, 128),
         vm(2, 2, HALO * 16, 128), vm(2, 1, HALO * 16, 128), vm(2, 2, HALO * 16, 128), vm(2, 1, HALO * 16, 128),
         vm(4, 512, 128),
         vm(R1 * 8, 128), vm(R1 * 8, 128), vm(R1 * 8, 128), vm(R1 * 8, 128),

time: 48.4 us -> 47.2 us (0.975)
  Pallas kernels: 46.8 us -> 45.6 us
    pallas_call x1, Pallas kernels: 46.8 us -> 45.6 us  [on_device(): pl.pallas_call(kernel, out_shape=pltpu.VMEM((2, 512, 128), F32), in_specs...]
where the time goes in v5:
time: 47.2 us; the launch traced here: 47.1 us
  Pallas kernels  45.6 us (97%)
  local copies, waits for them, and re-layouts  0.82 us (2%)
  between operations  0.64 us (1%)
    pallas_call x1, Pallas kernels, on_device(): pl.pallas_call(kernel, out_shape=pltpu.VMEM((2, 512, 128), F32), in_specs...  45.6 us

profile of v5, /device:TPU:0, one launch (start us, length us, event | category | flops | bytes accessed | tf_op | source)
XLA Modules:
  0.0 47.1 jit_solution(6311975680633762155)
XLA Ops:
  0.6 45.6 %shard_map.50 = f32[2,512,128]{2,1,0:T(8,128)S(1)} custom-call(f32[512,128]{1,0:T(8,128)} %bitcast.4, f32[512,128]{1,0:T(8,128)} %bitcast.5, s32[1,16]{1,0:T(1,128)} %own_hbm.1), custom_call_target="tpu_custom_call" | custom-call | tf_op jit(solution)/shard_map/pallas_call | solution.py:798
  46.3 0.8 %fusion = (f32[1,512,128]{2,1,0:T(8,128)}, f32[1,512,128]{2,1,0:T(8,128)}) fusion(f32[2,512,128]{2,1,0:T(8,128)S(1)} %shard_map.50), kind=kLoop, calls=%fused_computation | loop fusion | bytes 1048576 | tf_op jit(solution)/shard_map/slice | solution.py:808

commit v6 on v5

--- a/solution.py
+++ b/solution.py
@@ -351,12 +351,12 @@
             n = n + (pltpu.roll(c, 1, 1) + pltpu.roll(c, 127, 1))
             put(k, c, n)
 
-    def sweep1(src, dst):
+    def sweep1(src, dst, first, count):
         def put(k, c, n):
-            row = pl.ds((4 + k) * 8, 8)
-            dst[pl.ds(wrow(4 + k + zero), 8), :] = 0.2 * c + l1g[row, :] * (l1b[row, :] + 0.5 * n)
-
-        stencil1(src, 4 + zero, 24, put)
+            row = pl.ds((first + k) * 8, 8)
+            dst[pl.ds(wrow(first + k + zero), 8), :] = 0.2 * c + l1g[row, :] * (l1b[row, :] + 0.5 * n)
+
+        stencil1(src, first + zero, count, put)
 
     def restrict1():
         parts = []
@@ -482,7 +482,7 @@
             lax.fori_loop(0, 48 // per, body, 0)
 
         def start1():
-            for r in range(4, 28):
+            for r in range(5, 27):
                 row = pl.ds(r * 8, 8)
                 l1v[pl.ds(wrow(r), 8), :] = l1g[row, :] * l1b[row, :]
 
@@ -603,8 +603,8 @@
         sweep0(y, x, src, 3, 50, 50)
         stage("defect0", defect0)
         stage("start1", start1)
-        stage("sweep1", lambda: sweep1(l1v, l1w))
-        sweep1(l1w, l1v)
+        sweep1(l1v, l1w, 6, 20)
+        sweep1(l1w, l1v, 7, 18)
         stage("defect1", defect1)
         stage("down1", down1)
         each_r2("start", 0, bufs, cyc)
@@ -627,9 +627,9 @@
         stage("up2", up2)
         each_r2("wait_recv", 1, bufs, cyc)
         stage("correct1", correct1)
-        sweep1(l1v, l1w)
-        sweep1(l1w, l1v)
-        sweep1(l1v, l1w)
+        sweep1(l1v, l1w, 4, 24)
+        sweep1(l1w, l1v, 5, 22)
+        sweep1(l1v, l1w, 6, 20)
         stage("correct0", correct0)
         stage("sweep0post", lambda: sweep0(x, y, src, 9, 38, 38))
         sweep0(y, x, src, 10, 36, 36)
@@ -723,11 +723,11 @@
     def next_z(i, c):
         for k in (0, 1):
             for t in (0, 1):
-                row = pl.ds(vrow(t, TOP - 2 + 2 * i + k), 16)
+                row = pl.ds(vrow(t, TOP - 1 + 2 * i + k), 16)
                 vc[row, :] = vb[row, :] - step0_16 * vc[row, :]
         return c
 
-    lax.fori_loop(0, 18, next_z, 0, unroll=18)
+    lax.fori_loop(0, 17, next_z, 0, unroll=17)
 
     def apply_second(i, acc):
         r = TOP + 32 * i

time: 47.2 us -> 47.1 us (level)
  no operation moved by 1% of the time
where the time goes in v6:
time: 47.1 us; the launch traced here: 47 us
  Pallas kernels  45.5 us (97%)
  local copies, waits for them, and re-layouts  0.82 us (2%)
  between operations  0.64 us (1%)
    pallas_call x1, Pallas kernels, on_device(): pl.pallas_call(kernel, out_shape=pltpu.VMEM((2, 512, 128), F32), in_specs...  45.5 us

profile of v6, /device:TPU:0, one launch (start us, length us, event | category | flops | bytes accessed | tf_op | source)
XLA Modules:
  0.0 47.0 jit_solution(12404671150276558819)
XLA Ops:
  0.6 45.5 %shard_map.50 = f32[2,512,128]{2,1,0:T(8,128)S(1)} custom-call(f32[512,128]{1,0:T(8,128)} %bitcast.4, f32[512,128]{1,0:T(8,128)} %bitcast.5, s32[1,16]{1,0:T(1,128)} %own_hbm.1), custom_call_target="tpu_custom_call" | custom-call | tf_op jit(solution)/shard_map/pallas_call | solution.py:798
  46.2 0.8 %fusion = (f32[1,512,128]{2,1,0:T(8,128)}, f32[1,512,128]{2,1,0:T(8,128)}) fusion(f32[2,512,128]{2,1,0:T(8,128)S(1)} %shard_map.50), kind=kLoop, calls=%fused_computation | loop fusion | bytes 1048576 | tf_op jit(solution)/shard_map/slice | solution.py:808
